TPU v7x, 256 devices: a whole 4x4x8 slice. The times are simulated.
256 devices in a mesh: tm: 8 (over x, core), height: 16 (over z, y_hi), dp: 2 (over y_lo).
Axes of the slice: x: 4, y: 4 (y_hi: 2, y_lo: 2; y = y_hi * 2 + y_lo), z: 8, core: 2. Of those that a mesh axis runs over, the one named last changes fastest.
Arguments:
- video_clip: bfloat16 [2, 16, 64, 32, 256], P('dp', 'tm', 'height'), may hold values from -6 to 6
- conv_weight: bfloat16 [3, 3, 3, 256, 256], replicated, may hold values from -0.078125 to 0.078125
- down_weight: bfloat16 [3, 3, 3, 256, 256], replicated, may hold values from -0.078125 to 0.078125
- output_grad: bfloat16 [2, 8, 32, 16, 256], P('dp', 'tm', 'height'), may hold values from -12 to 12
Outputs:
- encoded: bfloat16 [2, 8, 32, 16, 256], P('dp', 'tm', 'height')
- clip_grad: bfloat16 [2, 16, 64, 32, 256], P('dp', 'tm', 'height')
- conv_grad: float32 [6912, 256], P(('height', 'dp'))
- down_grad: float32 [6912, 256], P(('height', 'dp'))
All inputs are finite; a program needn't handle non-finite values.
Results may differ from a plain program's by a relative error of at most 0.005.
Values may be sent and summed in bfloat16 or wider, within the bound.
A program may use at most 128 MiB of HBM per device.

v0:
```python
import math

import jax
import jax.numpy as jnp
from jax import lax
from jax.sharding import PartitionSpec as P


def shifted(block, axis, distance):
    devices = range(lax.axis_size(axis))
    route = [(i - distance, i) for i in devices if i - distance in devices]
    return lax.ppermute(block, axis, route)


def with_halo(cells, sides, width):
    for axis, dim in sides:
        count = lax.axis_size(axis)
        ends = count - 1
        head = lax.slice_in_dim(cells, 0, width, axis=dim)
        tail = lax.slice_in_dim(cells, cells.shape[dim] - width, cells.shape[dim], axis=dim)
        cells = jnp.concatenate(
            [
                lax.ppermute(tail, axis, [(i, (i + 1) % count) for i in range(ends)]),
                cells,
                lax.ppermute(head, axis, [((i + 1) % count, i) for i in range(ends)]),
            ],
            axis=dim,
        )
    return cells


def window_of(padded, time_tap, row_tap, stride, frame_count, row_count, column_count):
    pieces = [
        padded[
            time_tap : time_tap + stride * frame_count : stride,
            row_tap : row_tap + stride * row_count : stride,
            column_tap : column_tap + stride * column_count : stride,
        ]
        for column_tap in range(3)
    ]
    return jnp.concatenate(pieces, axis=-1).reshape(frame_count * row_count * column_count, -1)


def tap_conv(padded, weight, stride, frame_count, row_count, column_count):
    channels = weight.shape[-1]
    accumulated = jnp.zeros((frame_count * row_count * column_count, channels), jnp.float32)
    for time_tap in range(3):
        for row_tap in range(3):
            window = window_of(
                padded, time_tap, row_tap, stride, frame_count, row_count, column_count
            )
            accumulated = accumulated + jnp.dot(
                window,
                weight[time_tap, row_tap].reshape(3 * channels, channels),
                preferred_element_type=jnp.float32,
            )
    return accumulated.reshape(frame_count, row_count, column_count, channels)


def weight_terms(padded, grad_rows, stride, frame_count, row_count, column_count):
    blocks = []
    for time_tap in range(3):
        for row_tap in range(3):
            window = window_of(
                padded, time_tap, row_tap, stride, frame_count, row_count, column_count
            )
            blocks.append(jnp.dot(window.T, grad_rows, preferred_element_type=jnp.float32))
    return jnp.concatenate(blocks, axis=0)


def spread_back(grad_rows, weight, stride, shape, frame_count, row_count, column_count):
    channels = weight.shape[-1]
    result = jnp.zeros(shape, jnp.float32)
    for time_tap in range(3):
        for row_tap in range(3):
            product = jnp.dot(
                grad_rows,
                weight[time_tap, row_tap].reshape(3 * channels, channels).T,
                preferred_element_type=jnp.float32,
            )
            product = product.reshape(frame_count, row_count, column_count, 3, channels)
            for column_tap in range(3):
                result = result.at[
                    time_tap : time_tap + stride * frame_count : stride,
                    row_tap : row_tap + stride * row_count : stride,
                    column_tap : column_tap + stride * column_count : stride,
                ].add(product[:, :, :, column_tap])
    return result


def extend_time(block, first):
    received = shifted(block, "tm", 1)
    repeated = jnp.concatenate([block[:1], block[:1]], axis=0)
    return jnp.concatenate([jnp.where(first, repeated, received), block], axis=0)


def fold_time(grads, first):
    front = grads[:2]
    remaining = grads[2:]
    returned = shifted(front, "tm", -1)
    remaining = remaining.at[-2:].add(returned)
    own_part = jnp.where(first, front[0] + front[1], jnp.zeros_like(front[0]))
    return remaining.at[0].add(own_part)


def body(video_clip, conv_weight, down_weight, output_grad):
    frames_in = video_clip[0]
    frame_count, row_count, column_count, channels = frames_in.shape
    half_frames = frame_count // 2
    half_rows = row_count // 2
    half_columns = column_count // 2
    first = lax.axis_index("tm") == 0
    extended = extend_time(frames_in, first)
    rimmed = with_halo(extended, (("height", 1),), 1)
    padded_in = jnp.pad(rimmed, ((0, 0), (0, 0), (1, 1), (0, 0)))
    before = tap_conv(padded_in, conv_weight, 1, frame_count, row_count, column_count)
    hidden = jax.nn.silu(before).astype(jnp.bfloat16)
    extended_hidden = extend_time(hidden, first)
    below = shifted(extended_hidden[:, :1], "height", -1)
    padded_hidden = jnp.pad(
        jnp.concatenate([extended_hidden, below], axis=1), ((0, 0), (0, 0), (0, 1), (0, 0))
    )
    encoded = tap_conv(padded_hidden, down_weight, 2, half_frames, half_rows, half_columns).astype(
        jnp.bfloat16
    )
    grad_rows = output_grad[0].reshape(-1, channels)
    down_terms = weight_terms(padded_hidden, grad_rows, 2, half_frames, half_rows, half_columns)
    padded_grad = spread_back(
        grad_rows, down_weight, 2, padded_hidden.shape, half_frames, half_rows, half_columns
    )
    padded_grad = padded_grad[:, :, :column_count]
    borrowed = shifted(padded_grad[:, row_count : row_count + 1], "height", 1)
    hidden_grad = padded_grad[:, :row_count].at[:, :1].add(borrowed)
    hidden_grad = fold_time(hidden_grad, first)
    sigmoid = jax.nn.sigmoid(before)
    before_grad = (hidden_grad * (sigmoid * (1.0 + before * (1.0 - sigmoid)))).astype(jnp.bfloat16)
    before_rows = before_grad.reshape(-1, channels)
    conv_terms = weight_terms(padded_in, before_rows, 1, frame_count, row_count, column_count)
    padded_in_grad = spread_back(
        before_rows, conv_weight, 1, padded_in.shape, frame_count, row_count, column_count
    )
    padded_in_grad = padded_in_grad[:, :, 1:-1]
    rim_rows = jnp.concatenate([padded_in_grad[:, :1], padded_in_grad[:, -1:]], axis=1)
    returned = with_halo(rim_rows, (("height", 1),), 1)
    inner_grad = padded_in_grad[:, 1:-1]
    inner_grad = inner_grad.at[:, :1].add(returned[:, :1])
    inner_grad = inner_grad.at[:, -1:].add(returned[:, -1:])
    clip_grad = fold_time(inner_grad, first).astype(jnp.bfloat16)
    shared = (
        lax.psum_scatter(conv_terms, ("height", "dp"), scatter_dimension=0, tiled=True),
        lax.psum_scatter(down_terms, ("height", "dp"), scatter_dimension=0, tiled=True),
    )
    conv_sum, down_sum = lax.psum((shared[0], shared[1]), "tm")
    cell_total = (
        lax.axis_size("dp")
        * lax.axis_size("tm")
        * lax.axis_size("height")
        * frame_count
        * row_count
        * column_count
    )
    conv_scale = 1.0 / math.sqrt(cell_total)
    down_scale = 1.0 / math.sqrt(cell_total // 8)
    return (encoded[None], clip_grad[None], conv_sum * conv_scale, down_sum * down_scale)


def solution(mesh):
    placed = (P("dp", "tm", "height", None, None), P(), P(), P("dp", "tm", "height", None, None))
    return jax.shard_map(
        body,
        mesh=mesh,
        in_specs=placed,
        out_specs=(
            P("dp", "tm", "height", None, None),
            P("dp", "tm", "height", None, None),
            P(("height", "dp"), None),
            P(("height", "dp"), None),
        ),
        check_vma=False,
    )
```

profile of v0, /device:TPU:1, one launch (start us, length us, event | category | flops | bytes accessed | tf_op | source)
XLA Modules:
  0.0 661.8 jit_solution(16174168133564034269)
XLA Ops:
  7.2 4.5 collective-permute-start
  26.3 2.5 scatter_fusion
  28.9 2.5 scatter_fusion.1
  31.4 2.5 scatter_fusion.2
  33.9 2.5 scatter_fusion.3
  36.5 2.5 scatter_fusion.4
  39.0 2.5 scatter_fusion.5
  41.6 2.5 scatter_fusion.6
  44.1 2.5 scatter_fusion.7
  46.7 2.5 scatter_fusion.8
  49.2 2.5 scatter_fusion.9
  51.7 2.5 scatter_fusion.10
  54.3 2.5 scatter_fusion.11
  56.8 2.7 scatter_fusion.12
  59.5 2.5 scatter_fusion.13
  62.1 2.5 scatter_fusion.14
  64.6 2.5 scatter_fusion.15
  67.2 2.5 scatter_fusion.16
  69.7 2.5 scatter_fusion.17
  72.3 2.5 scatter_fusion.18
  74.8 2.5 scatter_fusion.19
  77.3 2.5 scatter_fusion.20
  79.9 2.5 scatter_fusion.21
  82.4 2.5 scatter_fusion.22
  85.0 2.5 scatter_fusion.23
  87.5 2.7 scatter_fusion.24
  90.3 2.5 scatter_fusion.25
  92.8 2.5 scatter_fusion.26
  95.4 4.8 collective-permute-start.5
  100.4 2.3 fusion.221
  102.8 3.3 collective-permute-start.1
  107.5 1.9 collective-permute-start.6
  109.5 3.7 collective-permute-done.2
  128.0 3.8 collective-permute-start.3
  131.7 1.9 collective-permute-done.3
  135.0 6.1 collective-permute-done.4
  159.9 2.0 fusion.87
  161.9 2.3 scatter-add.389
  179.7 5.8 collective-permute-start.7
  185.5 2.4 fusion.220
  189.3 7.5 %collective-permute-done.8 = f32[4,1,32,256]{3,2,1,0:T(8,128)S(1)} collective-permute-done((f32[4,1,32,256]{3,2,1,0:T(8,128)S(1)}, f32[4,1,32,256]{3,2,1,0:T(8,128)S(1)}, u32[]{:S(2)}, u32[]{:S(2)}) %collective-permute-start.8) | collective-permute-done | bytes 131104 | tf_op jit(solution)/shard_map/ppermute | solution.py:25
  196.9 2.3 collective-permute-start.9
  201.6 4.9 collective-permute-done.9
  206.7 148.1 %reduce-scatter.3.cloned.1.call-done = f32[216,256]{1,0:T(8,128)} async-done(((f32[6912,256]{1,0:T(8,128)}), f32[216,256]{1,0:T(8,128)}) %reduce-scatter.3.cloned.1.call-update) | async-done | bytes 221200 | tf_op jit(solution)/shard_map/reduce_scatter | solution.py:150
  354.8 228.6 %reduce-scatter.5.cloned.1.call-done = f32[216,256]{1,0:T(8,128)} async-done(((f32[6912,256]{1,0:T(8,128)}), f32[216,256]{1,0:T(8,128)}) %reduce-scatter.5.cloned.1.call-update) | async-done | bytes 221200 | tf_op jit(solution)/shard_map/reduce_scatter | solution.py:151
  584.0 67.5 %all-reduce.6.cloned.1.call-done = (f32[216,256]{1,0:T(8,128)}, f32[216,256]{1,0:T(8,128)}) async-done(((f32[216,256]{1,0:T(8,128)}, f32[216,256]{1,0:T(8,128)}), (f32[216,256]{1,0:T(8,128)}, f32[216,256]{1,0:T(8,128)})) %all-reduce.6.cloned.1.call-update) | async-done | bytes 442384 | tf_op jit(solution)/shard_map/psum | solution.py:153
  651.5 1.6 broadcast_multiply_fusion.1
  653.1 1.6 broadcast_multiply_fusion
  (257 shorter events, 70.1 us)
Async XLA Ops:
  7.2 5.2 copy-start
  7.2 347.6 %reduce-scatter.3.cloned.1.call-start = ((), (), s32[]{:S(2)}) async-start(), calls=%async_computation.2 | async-start | bytes 7299072 | tf_op jit(solution)/shard_map/reduce_scatter | solution.py:150
  7.2 95.5 %collective-permute-start = (bf16[2,4,32,256]{3,2,1,0:T(8,128)(2,1)}, bf16[2,4,32,256]{3,2,1,0:T(8,128)(2,1)S(1)}, u32[]{:S(2)}, u32[]{:S(2)}) collective-permute-start(bf16[2,4,32,256]{3,2,1,0:T(8,128)(2,1)} %bitcast.609), channel_id=1, source_target_pairs={{0,32},{32,64},{64,96},{96,128},{128,160},{160,192},{192,224},{1,3... | collective-permute-start | bytes 393224 | tf_op jit(solution)/shard_map/ppermute | solution.py:12
  77.3 25.4 %copy-start.1 = (bf16[1,2,4,32,256]{4,3,2,1,0:T(8,128)(2,1)S(1)}, bf16[1,2,4,32,256]{4,3,2,1,0:T(8,128)(2,1)}, u32[]{:S(2)}) copy-start(bf16[1,2,4,32,256]{4,3,2,1,0:T(8,128)(2,1)} %param.76) | copy-start | bytes 393220
  95.4 12.0 %collective-permute-start.5 = (f32[4,1,32,256]{3,2,1,0:T(8,128)S(1)}, f32[4,1,32,256]{3,2,1,0:T(8,128)S(1)}, u32[]{:S(2)}, u32[]{:S(2)}) collective-permute-start(f32[4,1,32,256]{3,2,1,0:T(8,128)S(1)} %copy.67), channel_id=1, source_target_pairs={{0,2},{2,4},{4,6},{6,8},{8,10},{10,12},{12,14},{14,16},{16,18},{18... | collective-permute-start | bytes 393224 | tf_op jit(solution)/shard_map/ppermute | solution.py:12
  102.8 6.6 %collective-permute-start.1 = (bf16[4,1,32,256]{3,2,1,0:T(8,128)(2,1)S(1)}, bf16[4,1,32,256]{3,2,1,0:T(8,128)(2,1)S(1)}, u32[]{:S(2)}, u32[]{:S(2)}) collective-permute-start(bf16[4,1,32,256]{3,2,1,0:T(8,128)(2,1)S(1)} %get-tuple-element.480), channel_id=1, source_target_pairs={{0,2},{2,4},{4,6},{6,8},{8,10},{10,12},{12,14},{14,16},{16,18},{18... | collective-permute-start | bytes 196616 | tf_op jit(solution)/shard_map/ppermute | solution.py:23
  106.2 7.0 %collective-permute-start.2 = (bf16[4,1,32,256]{3,2,1,0:T(8,128)(2,1)S(1)}, bf16[4,1,32,256]{3,2,1,0:T(8,128)(2,1)S(1)}, u32[]{:S(2)}, u32[]{:S(2)}) collective-permute-start(bf16[4,1,32,256]{3,2,1,0:T(8,128)(2,1)S(1)} %get-tuple-element.481), channel_id=1, source_target_pairs={{2,0},{4,2},{6,4},{8,6},{10,8},{12,10},{14,12},{16,14},{18,16},{20... | collective-permute-start | bytes 196616 | tf_op jit(solution)/shard_map/ppermute | solution.py:25
  107.5 9.2 %collective-permute-start.6 = (f32[2,4,32,256]{3,2,1,0:T(8,128)S(1)}, f32[2,4,32,256]{3,2,1,0:T(8,128)S(1)}, u32[]{:S(2)}, u32[]{:S(2)}) collective-permute-start(f32[2,4,32,256]{3,2,1,0:T(8,128)S(1)} %slice.2233), channel_id=1, source_target_pairs={{32,0},{64,32},{96,64},{128,96},{160,128},{192,160},{224,192},{33,... | collective-permute-start | bytes 786440 | tf_op jit(solution)/shard_map/ppermute | solution.py:12
  127.9 455.4 %reduce-scatter.5.cloned.1.call-start = ((), (), s32[]{:S(2)}) async-start(), calls=%async_computation.3 | async-start | bytes 7299072 | tf_op jit(solution)/shard_map/reduce_scatter | solution.py:151
  128.0 5.7 collective-permute-start.3
  133.7 7.4 %collective-permute-start.4 = (bf16[4,1,32,256]{3,2,1,0:T(8,128)(2,1)S(1)}, bf16[4,1,32,256]{3,2,1,0:T(8,128)(2,1)S(1)}, u32[]{:S(2)}, u32[]{:S(2)}) collective-permute-start(bf16[4,1,32,256]{3,2,1,0:T(8,128)(2,1)S(1)} %pad_maximum_fusion.9), channel_id=1, source_target_pairs={{2,0},{4,2},{6,4},{8,6},{10,8},{12,10},{14,12},{16,14},{18,16},{20... | collective-permute-start | bytes 196616 | tf_op jit(solution)/shard_map/ppermute | solution.py:12
  154.9 496.6 %all-reduce.6.cloned.1.call-start = ((), (), s32[]{:S(2)}) async-start(), calls=%async_computation.4 | async-start | bytes 884736 | tf_op jit(solution)/shard_map/psum | solution.py:153
  179.7 9.5 %collective-permute-start.7 = (f32[4,1,32,256]{3,2,1,0:T(8,128)S(1)}, f32[4,1,32,256]{3,2,1,0:T(8,128)S(1)}, u32[]{:S(2)}, u32[]{:S(2)}) collective-permute-start(f32[4,1,32,256]{3,2,1,0:T(8,128)S(1)} %get-tuple-element.449), channel_id=1, source_target_pairs={{0,2},{2,4},{4,6},{6,8},{8,10},{10,12},{12,14},{14,16},{16,18},{18... | collective-permute-start | bytes 393224 | tf_op jit(solution)/shard_map/ppermute | solution.py:23
  188.0 8.9 %collective-permute-start.8 = (f32[4,1,32,256]{3,2,1,0:T(8,128)S(1)}, f32[4,1,32,256]{3,2,1,0:T(8,128)S(1)}, u32[]{:S(2)}, u32[]{:S(2)}) collective-permute-start(f32[4,1,32,256]{3,2,1,0:T(8,128)S(1)} %get-tuple-element.448), channel_id=1, source_target_pairs={{2,0},{4,2},{6,4},{8,6},{10,8},{12,10},{14,12},{16,14},{18,16},{20... | collective-permute-start | bytes 393224 | tf_op jit(solution)/shard_map/ppermute | solution.py:25
  196.9 9.7 %collective-permute-start.9 = (f32[2,4,32,256]{3,2,1,0:T(8,128)S(1)}, f32[2,4,32,256]{3,2,1,0:T(8,128)S(1)}, u32[]{:S(2)}, u32[]{:S(2)}) collective-permute-start(f32[2,4,32,256]{3,2,1,0:T(8,128)S(1)} %slice.2294), channel_id=1, source_target_pairs={{32,0},{64,32},{96,64},{128,96},{160,128},{192,160},{224,192},{33,... | collective-permute-start | bytes 786440 | tf_op jit(solution)/shard_map/ppermute | solution.py:12
Sparse Core Ops, SparseCore 0:
  128.0 226.6 reduce-scatter.2
  359.3 223.9 reduce-scatter.4
  585.8 65.6 all-reduce.5
where the time goes:
time: 674 us; the launch traced here: 662 us
  waiting for transfers between devices  468 us (69%)
  other arithmetic  77.5 us (11%)
  matrix products  49.4 us (7%)
  starting transfers between devices  30.4 us (5%)
  local copies, waits for them, and re-layouts  20.2 us (3%)
  between operations  15.8 us (2%)
    reduce_scatter x1, waiting for transfers between devices, body(): lax.psum_scatter(down_terms, ('height', 'dp'), scatter_dimension=0, tiled...  229 us
    reduce_scatter x1, waiting for transfers between devices, body(): lax.psum_scatter(conv_terms, ('height', 'dp'), scatter_dimension=0, tiled...  148 us
    scatter-add x35, other arithmetic, spread_back(): result = result.at[time_tap:time_tap + stride * frame_count:stride, row_t...  69.3 us
    psum x1, waiting for transfers between devices, body(): conv_sum, down_sum = lax.psum((shared[0], shared[1]), 'tm')  67.5 us
    dot_general x18, matrix products, spread_back(): jnp.dot(grad_rows, weight[time_tap, row_tap].reshape(3 * channels, channe...  23 us
    dot_general x18, matrix products, weight_terms(): jnp.dot(window.T, grad_rows, preferred_element_type=jnp.float32)  21.7 us
    ppermute x6, starting transfers between devices, shifted(): return lax.ppermute(block, axis, route)  18.6 us
  transfers between devices with their start and end apart: 13, of which 8 were waited for; matrix products, arithmetic and copies ran while one was open for 20% of the time, Pallas kernels for 0%

commit v1 on v0

v1 whole, which is shorter than its diff:
```python
import functools
import math

import jax
import jax.numpy as jnp
from jax import lax
from jax.experimental import pallas as pl
from jax.experimental.pallas import tpu as pltpu
from jax.sharding import PartitionSpec as P

MESH = pl.DeviceIdType.MESH
F32 = jnp.float32
BF16 = jnp.bfloat16
NT = (((1,), (1,)), ((), ()))
TN = (((0,), (0,)), ((), ()))


def iota2(shape, dim):
    return lax.broadcasted_iota(jnp.int32, shape, dim)


def one_hot(mask):
    return jnp.where(mask, 1.0, 0.0).astype(F32).astype(BF16)


def column_order(n):
    m, k = iota2((n, n), 0), iota2((n, n), 1)
    return one_hot(k == (m & ~31) + 2 * (m & 15) + ((m >> 4) & 1))


def channel_order(n):
    i, k = iota2((n, n), 0), iota2((n, n), 1)
    j = k & 127
    return one_hot(i == (j >> 3) * 16 + (k >> 7) * 8 + (j & 7))


def move_in_16(x, step):
    n = x.shape[0]
    k = iota2(x.shape, 0) & 15
    rolled = pltpu.roll(x, step % n, 0)
    return jnp.where(k == (0 if step == 1 else 15), 0.0, rolled)


def halves(x):
    groups = x.shape[0] // 32
    parts = x.reshape(groups, 2, 16, x.shape[1])
    return parts[:, 0].reshape(groups * 16, -1), parts[:, 1].reshape(groups * 16, -1)


def joined(even, odd):
    groups = even.shape[0] // 16
    parts = [h.reshape(groups, 1, 16, h.shape[1]) for h in (even, odd)]
    return jnp.concatenate(parts, axis=1).reshape(groups * 32, -1)


def from_left(x):
    even, odd = halves(x)
    return joined(move_in_16(odd, 1), even)


def from_right(x):
    even, odd = halves(x)
    return joined(odd, move_in_16(even, -1))


def kernel(
    sizes,
    x_ref, w1_hbm, w2_hbm, og_ref,
    enc_ref, clip_ref, conv_ref, down_ref,
    w1, w2, xe, oge, he, ge, hg, before, zs,
    xs, gs, hs, os_, xg, gg, hgat, ogat, xt, g3, part,
    sl, r1, s1, r2, fs, fg, ff,
    wsem, p1s, p1r, p2s, p2r,
    xss, xsr, gss, gsr, hss, hsr, oss, osr,
    rs1s, rs1r, rs2s, rs2r, ags, agr,
):
    nt, nh, nd = sizes
    ny, nz = 2 * nd, nh // 2
    t, h, d = lax.axis_index("tm"), lax.axis_index("height"), lax.axis_index("dp")
    y, z = (h % 2) * nd + d, h // 2
    core, chip = t % 2, t // 2
    t_next, t_prev = (t + 1) % nt, (t + nt - 1) % nt
    h_next, h_prev = (h + 1) % nh, (h + nh - 1) % nh
    block = z * ny + y
    groups = 864 // (ny * nz)
    slot = 8 * ((groups + 1) // 2)

    wc1 = pltpu.make_async_copy(w1_hbm, w1, wsem.at[0])
    wc2 = pltpu.make_async_copy(w2_hbm, w2, wsem.at[1])
    wc2.start()
    wc1.start()

    def at_y(k):
        return (t, z * 2 + k // nd, k % nd)

    barrier = pltpu.get_barrier_semaphore()

    def greet(where):
        pl.semaphore_signal(barrier, inc=1, device_id=where, device_id_type=MESH)

    for k in range(1, nt):
        greet(((t + k) % nt, h, d))
    for hh in (h_next, h_prev):
        for tt in (t_prev, t, t_next):
            greet((tt, hh, d))
    for k in range(1, ny):
        greet(at_y((y + k) % ny))
    for k in range(1, nz):
        greet((t, ((z + k) % nz) * 2 + h % 2, d))

    x_own = jnp.dot(column_order(256), x_ref[...], preferred_element_type=F32).astype(BF16)
    xe[2:4, 1:5] = x_own.reshape(2, 4, 32, 256)
    oge[0, 1:3] = og_ref[...].reshape(2, 16, 256)
    for k in range(2):
        os_[k] = og_ref[:, 128 * k : 128 * (k + 1)].reshape(2, 16, 128)

    pl.semaphore_wait(barrier, (nt - 1) + 6 + (ny - 1) + (nz - 1))

    def send(src, dst, ssem, rsem, where):
        return pltpu.make_async_remote_copy(
            src_ref=src, dst_ref=dst, send_sem=ssem, recv_sem=rsem, device_id=where, device_id_type=MESH
        )

    def p1(k, src, dst, where):
        return send(src, dst, p1s.at[k], p1r.at[k], where)

    og_halo = [
        p1(0, oge.at[0:1, 1:3], oge.at[1:2, 1:3], (t_prev, h, d)),
        p1(1, oge.at[0:1, 2:3], oge.at[0:1, 0:1], (t, h_next, d)),
        p1(2, oge.at[0:1, 2:3], oge.at[1:2, 0:1], (t_prev, h_next, d)),
    ]
    x_halo = [
        p1(3, xe.at[2:4, 1:5], xe.at[0:2, 1:5], (t_next, h, d)),
        p1(4, xe.at[2:4, 4:5], xe.at[2:4, 0:1], (t, h_next, d)),
        p1(5, xe.at[2:4, 1:2], xe.at[2:4, 5:6], (t, h_prev, d)),
        p1(6, xe.at[2:4, 4:5], xe.at[0:2, 0:1], (t_next, h_next, d)),
        p1(7, xe.at[2:4, 1:2], xe.at[0:2, 5:6], (t_next, h_prev, d)),
    ]
    for c in og_halo + x_halo:
        c.start()

    def gather_sends(role, source, target, ssem, rsem):
        for k in range(nt // 2):
            to_chip = (chip + k) % (nt // 2)
            to = to_chip * 2 + role
            c = send(source(to_chip), target(t), ssem.at[k], rsem.at[t], (to, h, d))
            if k == 0:
                pl.when(core != role)(c.start)
            else:
                c.start()

    def gather_sent(role, source, target, ssem, rsem):
        for k in range(nt // 2):
            to_chip = (chip + k) % (nt // 2)
            c = send(source(to_chip), target(t), ssem.at[k], rsem.at[t], (to_chip * 2 + role, h, d))
            if k == 0:
                pl.when(core != role)(c.wait_send)
            else:
                c.wait_send()

    def gather_received(source, target, ssem, rsem):
        for k in range(1, nt):
            s = (t + k) % nt
            send(source(0), target(s), ssem.at[0], rsem.at[s], (s, h, d)).wait_recv()

    og_move = (lambda c: os_.at[c % 2], lambda s: ogat.at[s], oss, osr)
    x_move = (lambda c: xs.at[c // 2], lambda s: xg.at[pl.ds(2 + 2 * s, 2)], xss, xsr)
    g_move = (lambda c: gs.at[c % 2], lambda s: gg.at[pl.ds(2 * s, 2)], gss, gsr)
    h_move = (lambda c: hs.at[c // 2], lambda s: hgat.at[pl.ds(2 + 2 * s, 2)], hss, hsr)
    gather_sends(1, *og_move)

    wc2.wait()
    for c in og_halo:
        c.wait_recv()

    @pl.when(t == nt - 1)
    def _():
        oge[1] = jnp.zeros((3, 16, 256), BF16)

    @pl.when(h == 0)
    def _():
        oge[:, 0] = jnp.zeros((2, 16, 256), BF16)

    og_rows = oge[...].reshape(96, 256)
    first = t == 0
    terms = {}
    for e in range(3):
        for a in range(3):
            for b in range(3):
                lhs = og_rows if a < 2 else og_rows[:48]
                q = lax.dot_general(lhs, w2[a * 9 + b * 3 + e], NT, preferred_element_type=F32)
                offset = 0 if b == 2 else 16
                here = q[offset : offset + 32]
                if a < 2:
                    here = jnp.where(first, here, 0.0)
                    later = q[48 + offset : 48 + offset + 32]
                    key = (a, b % 2, e)
                    terms[key] = terms.get(key, 0.0) + later
                key = (0, b % 2, e)
                terms[key] = terms.get(key, 0.0) + here
    for f in range(2):
        for b in range(2):
            even = terms[f, b, 0] + move_in_16(terms[f, b, 2], 1)
            odd = terms[f, b, 1]
            for u in range(2):
                hg[f, 2 * u + b, 0:16] = even[16 * u : 16 * u + 16]
                hg[f, 2 * u + b, 16:32] = odd[16 * u : 16 * u + 16]

    for c in x_halo:
        c.wait_recv()

    @pl.when(h == 0)
    def _():
        xe[:, 0] = jnp.zeros((4, 32, 256), BF16)

    @pl.when(h == nh - 1)
    def _():
        xe[:, 5] = jnp.zeros((4, 32, 256), BF16)

    @pl.when(first)
    def _():
        xe[0] = xe[2]
        xe[1] = xe[2]

    by_channel = channel_order(256)
    moved = jnp.dot(xe[2:4].reshape(384, 256), by_channel, preferred_element_type=F32).astype(BF16)
    for k in range(2):
        xs[k] = moved[:, 128 * k : 128 * (k + 1)].reshape(2, 6, 32, 128)
    gather_sends(0, *x_move)

    wc1.wait()
    sums = [None] * 3
    for a in range(3):
        for b in range(3):
            lhs = xe[a : a + 2, b : b + 4].reshape(256, 256)
            for e in range(3):
                q = jnp.dot(lhs, w1[a * 9 + b * 3 + e], preferred_element_type=F32)
                sums[e] = q if sums[e] is None else sums[e] + q
    value = from_left(sums[0]) + sums[1] + from_right(sums[2])
    sigmoid = jax.nn.sigmoid(value)
    he[2:4, 0:4] = (value * sigmoid).astype(BF16).reshape(2, 4, 32, 256)
    slope = sigmoid * (1.0 + value * (1.0 - sigmoid))
    grad = (hg[...].reshape(256, 256) * slope).astype(BF16)
    ge[0:2, 1:5] = grad.reshape(2, 4, 32, 256)
    for k in range(2):
        gs[k] = grad[:, 128 * k : 128 * (k + 1)].reshape(2, 4, 32, 128)

    def p2(k, src, dst, where):
        return send(src, dst, p2s.at[k], p2r.at[k], where)

    h_rows = p2(0, he.at[2:4, 0:1], he.at[2:4, 4:5], (t, h_prev, d))
    h_halo = [
        p2(1, he.at[2:4, 0:1], he.at[0:2, 4:5], (t_next, h_prev, d)),
        p2(2, he.at[2:4, 0:4], he.at[0:2, 0:4], (t_next, h, d)),
    ]
    g_halo = [
        p2(3, ge.at[0:2, 1:5], ge.at[2:4, 1:5], (t_prev, h, d)),
        p2(4, ge.at[0:2, 4:5], ge.at[0:2, 0:1], (t, h_next, d)),
        p2(5, ge.at[0:2, 1:2], ge.at[0:2, 5:6], (t, h_prev, d)),
        p2(6, ge.at[0:2, 4:5], ge.at[2:4, 0:1], (t_prev, h_next, d)),
        p2(7, ge.at[0:2, 1:2], ge.at[2:4, 5:6], (t_prev, h_prev, d)),
    ]
    h_rows.start()
    gather_sends(0, *g_move)
    for c in h_halo + g_halo:
        c.start()
    h_rows.wait_recv()

    @pl.when(h == nh - 1)
    def _():
        he[2:4, 4] = jnp.zeros((2, 32, 256), BF16)

    moved = jnp.dot(he[2:4].reshape(320, 256), by_channel, preferred_element_type=F32).astype(BF16)
    for k in range(2):
        hs[k] = moved[:, 128 * k : 128 * (k + 1)].reshape(2, 5, 32, 128)
    gather_sends(1, *h_move)

    for c in h_halo:
        c.wait_recv()

    @pl.when(h == nh - 1)
    def _():
        he[0:2, 4] = jnp.zeros((2, 32, 256), BF16)

    @pl.when(first)
    def _():
        he[0] = he[2]
        he[1] = he[2]

    sums = [None] * 3
    for a in range(3):
        for b in range(3):
            for e in range(3):
                p = 16 * (e % 2)
                lhs = jnp.concatenate([he[a, b, p : p + 16], he[a, b + 2, p : p + 16]], axis=0)
                q = jnp.dot(lhs, w2[a * 9 + b * 3 + e], preferred_element_type=F32)
                sums[e] = q if sums[e] is None else sums[e] + q
    enc_ref[...] = (sums[0] + sums[1] + move_in_16(sums[2], -1)).astype(BF16)

    part[pl.ds(27 * 128, 8)] = jnp.zeros((8, 128), F32)

    @pl.when(core == 0)
    def _():
        xg[pl.ds(2 + 2 * t, 2)] = xs[chip // 2]
        gg[pl.ds(2 * t, 2)] = gs[chip % 2]
        gather_received(*x_move)
        xg[0] = xg[2]
        xg[1] = xg[2]

        def turn(f, carry):
            for b in range(3):
                xt[f, 128 * b : 128 * (b + 1)] = xg[f, b : b + 4].reshape(128, 128).T
            return carry

        lax.fori_loop(0, 2 * nt + 2, turn, 0)
        gather_received(*g_move)

        def spread(s, carry):
            rows = pl.ds(pl.multiple_of(256 * s, 256), 256)
            g = gg[pl.ds(2 * s, 2)].reshape(256, 128)
            wide = g.astype(F32)
            g3[rows, 0:128] = from_right(wide).astype(BF16)
            g3[rows, 128:256] = g
            g3[rows, 256:384] = from_left(wide).astype(BF16)
            return carry

        lax.fori_loop(0, nt, spread, 0)
        for a in range(3):
            lhs = jnp.concatenate([xt[a + f] for f in range(2 * nt)], axis=1)
            q = jnp.dot(lhs, g3[...], preferred_element_type=F32)
            for b in range(3):
                for e in range(3):
                    n = 128 * (a * 9 + b * 3 + e)
                    part[n : n + 128] = q[128 * b : 128 * (b + 1), 128 * e : 128 * (e + 1)]

    @pl.when(core == 1)
    def _():
        hgat[pl.ds(2 + 2 * t, 2)] = hs[chip // 2]
        ogat[t] = os_[chip % 2]
        gather_received(*og_move)
        gather_received(*h_move)
        hgat[0] = hgat[2]
        hgat[1] = hgat[2]
        og_all = ogat[...].reshape(32 * nt, 128)
        og_two = jnp.concatenate([og_all, move_in_16(og_all.astype(F32), 1).astype(BF16)], axis=1)
        for a in range(3):
            for b in range(3):
                for p in range(2):
                    lhs = jnp.concatenate(
                        [
                            hgat[2 * f + a, 2 * r + b, 16 * p : 16 * p + 16]
                            for f in range(nt)
                            for r in range(2)
                        ],
                        axis=0,
                    )
                    q = lax.dot_general(
                        lhs, og_all if p else og_two, TN, preferred_element_type=F32
                    )
                    n = 128 * (a * 9 + b * 3)
                    if p:
                        part[n + 128 : n + 256] = q
                    else:
                        part[n : n + 128] = q[:, :128]
                        part[n + 256 : n + 384] = q[:, 128:]

    half = chip // 2

    def cut(k, carry):
        start = (groups * k + 1 - half) // 2
        rows = part[pl.ds(pl.multiple_of(start * 8, 8), slot)]
        sl[k % ny, k // ny] = rows.astype(BF16)
        return carry

    lax.fori_loop(0, ny * nz, cut, 0)
    y_sends = []
    for k in range(1, ny):
        to = (y + k) % ny
        y_sends.append(send(sl.at[to], r1.at[k - 1], rs1s.at[k - 1], rs1r.at[k - 1], at_y(to)))
    for c in y_sends:
        c.start()

    for c in g_halo:
        c.wait_recv()

    @pl.when(t == nt - 1)
    def _():
        ge[2:4] = jnp.zeros((2, 6, 32, 256), BF16)

    @pl.when(h == 0)
    def _():
        ge[:, 0] = jnp.zeros((4, 32, 256), BF16)

    @pl.when(h == nh - 1)
    def _():
        ge[:, 5] = jnp.zeros((4, 32, 256), BF16)

    sums = [None] * 3
    for a in range(3):
        for b in range(3):
            lhs = ge[2 - a : 4 - a, 2 - b : 6 - b].reshape(256, 256)
            for e in range(3):
                q = lax.dot_general(lhs, w1[a * 9 + b * 3 + e], NT, preferred_element_type=F32)
                sums[e] = q if sums[e] is None else sums[e] + q
    for e in range(3):
        zs[e] = sums[e]

    @pl.when(first)
    def _():
        for e in range(3):
            total = zs[e, 0:128]
            for a, f in ((0, 0), (0, 1), (1, 0)):
                for b in range(3):
                    lhs = ge[f, 2 - b : 6 - b].reshape(128, 256)
                    total = total + lax.dot_general(
                        lhs, w1[a * 9 + b * 3 + e], NT, preferred_element_type=F32
                    )
            zs[e, 0:128] = total

    clip = (from_right(zs[0]) + zs[1] + from_left(zs[2])).astype(BF16)
    clip_ref[...] = lax.dot_general(
        column_order(256), clip, TN, preferred_element_type=F32
    ).astype(BF16)

    for c in y_sends:
        c.wait_recv()

    def add_y(k, carry):
        total = sl[y, k].astype(F32)
        for n in range(ny - 1):
            total = total + r1[n, k].astype(F32)
        s1[k] = total.astype(BF16)
        return carry

    lax.fori_loop(0, nz, add_y, 0)
    z_sends = []
    for k in range(1, nz):
        to = (z + k) % nz
        where = (t, to * 2 + h % 2, d)
        z_sends.append(send(s1.at[to], r2.at[k - 1], rs2s.at[k - 1], rs2r.at[k - 1], where))
    for c in z_sends:
        c.start()
    total = s1[z].astype(F32)
    for k, c in enumerate(z_sends):
        c.wait_recv()
        total = total + r2[k].astype(F32)
    fs[...] = total.astype(BF16)
    t_sends = []
    for k in range(1, nt):
        where = ((t + k) % nt, h, d)
        t_sends.append(send(fs, fg.at[t], ags.at[k - 1], agr.at[k - 1], where))
    for c in t_sends:
        c.start()
    fg[t] = fs[...]
    for k in range(1, nt):
        s = (t + nt - k) % nt
        send(fs, fg.at[s], ags.at[k - 1], agr.at[k - 1], (s, h, d)).wait_recv()

    cells = sizes[0] * sizes[1] * sizes[2] * 256
    scale = (1.0 / math.sqrt(cells), 1.0 / math.sqrt(cells // 8))
    for s in range(nt):
        ff[s] = fg[s].astype(F32) * scale[s % 2]
    for j in range(groups):
        parity = (groups * block + j) % 2
        for o in range(2):
            for k, out in enumerate((conv_ref, down_ref)):
                source = 2 * (2 * parity + o) + k
                out[8 * j : 8 * j + 8, 128 * o : 128 * o + 128] = ff[
                    source, 8 * (j // 2) : 8 * (j // 2) + 8
                ]

    for c in og_halo + x_halo + [h_rows] + h_halo + g_halo + y_sends + z_sends + t_sends:
        c.wait_send()
    gather_sent(1, *og_move)
    gather_sent(0, *x_move)
    gather_sent(0, *g_move)
    gather_sent(1, *h_move)


def body(mesh_sizes, video_clip, conv_weight, down_weight, output_grad):
    nt, nh, nd = mesh_sizes
    ny, nz = 2 * nd, nh // 2
    blocks = ny * nz
    groups = 864 // blocks
    slot = 8 * ((groups + 1) // 2)
    dma = pltpu.SemaphoreType.DMA

    def vm(*shape, dtype=BF16):
        return pltpu.VMEM(shape, dtype)

    scratch = [
        vm(27, 256, 256), vm(27, 256, 256),
        vm(4, 6, 32, 256), vm(2, 3, 16, 256), vm(4, 5, 32, 256), vm(4, 6, 32, 256),
        vm(2, 4, 32, 256, dtype=F32), vm(256, 256, dtype=F32), vm(3, 256, 256, dtype=F32),
        vm(2, 2, 6, 32, 128), vm(2, 2, 4, 32, 128), vm(2, 2, 5, 32, 128), vm(2, 2, 16, 128),
        vm(2 * nt + 2, 6, 32, 128), vm(2 * nt, 4, 32, 128),
        vm(2 * nt + 2, 5, 32, 128), vm(nt, 2, 16, 128),
        vm(2 * nt + 2, 384, 128), vm(256 * nt, 384), vm(27 * 128 + 8, 128, dtype=F32),
        vm(ny, nz, slot, 128), vm(ny - 1, nz, slot, 128),
        vm(nz, slot, 128), vm(nz - 1, slot, 128),
        vm(slot, 128), vm(nt, slot, 128), vm(nt, slot, 128, dtype=F32),
        dma((2,)), dma((8,)), dma((8,)), dma((8,)), dma((8,)),
    ]
    scratch += [dma((n,)) for _ in range(4) for n in (nt // 2, nt)]
    scratch += [dma((n,)) for n in (ny - 1, ny - 1, nz - 1, nz - 1, nt - 1, nt - 1)]
    vmem = pl.BlockSpec(memory_space=pltpu.VMEM)
    hbm = pl.BlockSpec(memory_space=pl.ANY)
    enc, clip, conv, down = pl.pallas_call(
        functools.partial(kernel, mesh_sizes),
        out_shape=(
            jax.ShapeDtypeStruct((32, 256), BF16),
            jax.ShapeDtypeStruct((256, 256), BF16),
            jax.ShapeDtypeStruct((groups * 8, 256), F32),
            jax.ShapeDtypeStruct((groups * 8, 256), F32),
        ),
        in_specs=[vmem, hbm, hbm, vmem],
        out_specs=(vmem,) * 4,
        scratch_shapes=scratch,
        compiler_params=pltpu.CompilerParams(
            collective_id=0, has_side_effects=True, vmem_limit_bytes=44 * 2**20
        ),
    )(
        video_clip.reshape(256, 256),
        conv_weight.reshape(27, 256, 256),
        down_weight.reshape(27, 256, 256),
        output_grad.reshape(32, 256),
    )
    return enc.reshape(1, 1, 2, 16, 256), clip.reshape(1, 2, 4, 32, 256), conv, down


def solution(mesh):
    sizes = tuple(mesh.shape[a] for a in ("tm", "height", "dp"))
    cells = P("dp", "tm", "height", None, None)
    rows = P(("height", "dp"), None)
    return jax.shard_map(
        functools.partial(body, sizes),
        mesh=mesh,
        in_specs=(cells, P(), P(), cells),
        out_specs=(cells, cells, rows, rows),
        check_vma=False,
    )
```

time: 674 us -> 67.3 us (0.10); the launches traced: 662 us -> 67.1 us
  waiting for transfers between devices: 468 us -> 0 us
  other arithmetic: 77.5 us -> 0 us
  Pallas kernels: 0 us -> 58.2 us
  matrix products: 49.4 us -> 0 us
  starting transfers between devices: 30.4 us -> 0 us
  between operations: 15.8 us -> 0.65 us
  local copies, waits for them, and re-layouts: 20.2 us -> 8.25 us
    reduce_scatter x2 -> x0, waiting for transfers between devices: 377 us -> none  [the longest x1 229 us: body(): lax.psum_scatter(down_terms, ('height', 'dp'), scatter_dimension=0, tiled...]
    scatter-add x40 -> x0, other arithmetic: 69.5 us -> none  [the longest x35 69.3 us: spread_back(): result = result.at[time_tap:time_tap + stride * frame_count:stride, row_t...]
    psum x1 -> x0, waiting for transfers between devices: 67.5 us -> none  [body(): conv_sum, down_sum = lax.psum((shared[0], shared[1]), 'tm')]
    pallas_call x0 -> x1, Pallas kernels: none -> 58.2 us  [body(): pl.pallas_call(functools.partial(kernel, mesh_sizes), out_shape=(jax.Shap...]
    dot_general x54 -> x0, matrix products: 49.4 us -> none  [the longest x18 23 us: spread_back(): jnp.dot(grad_rows, weight[time_tap, row_tap].reshape(3 * channels, channe...]
    ppermute x10 -> x0, starting transfers between devices: 30.3 us -> none  [the longest x6 18.6 us: shifted(): return lax.ppermute(block, axis, route)]
    ppermute x10 -> x0, waiting for transfers between devices: 24.2 us -> none  [the longest x6 12.9 us: shifted(): return lax.ppermute(block, axis, route)]
    scatter-add x19 -> x0, local copies, waits for them, and re-layouts: 8.84 us -> none  [spread_back(): result = result.at[time_tap:time_tap + stride * frame_count:stride, row_t...]
  transfers between devices with their start and end apart: 13 -> 0, of which waited for: 8 -> 0; matrix products, arithmetic and copies ran while one was open for 20% -> 0% of each run, Pallas kernels for 0% -> 0%
where the time goes in v1:
time: 67.3 us; the launch traced here: 67.1 us
  Pallas kernels  58.2 us (86%)
  local copies, waits for them, and re-layouts  8.25 us (12%)
    pallas_call x1, Pallas kernels, body(): pl.pallas_call(functools.partial(kernel, mesh_sizes), out_shape=(jax.Shap...  58.2 us
    unnamed x12, local copies, waits for them, and re-layouts  8.25 us

profile of v1, /device:TPU:1, one launch (start us, length us, event | category | flops | bytes accessed | tf_op | source)
XLA Modules:
  0.0 67.1 jit_solution(9956640298195187586)
XLA Ops:
  0.6 0.0 copy-start
  0.6 2.0 %copy-done = bf16[3,3,3,256,256]{4,3,2,1,0:T(8,128)(2,1)S(1)} copy-done((bf16[3,3,3,256,256]{4,3,2,1,0:T(8,128)(2,1)S(1)}, bf16[3,3,3,256,256]{4,3,2,1,0:T(8,128)(2,1)}, u32[]{:S(2)}) %copy-start) | copy-done | bytes 3538968
  2.6 0.0 copy-start.1
  2.6 2.0 %copy-done.1 = bf16[3,3,3,256,256]{4,3,2,1,0:T(8,128)(2,1)S(1)} copy-done((bf16[3,3,3,256,256]{4,3,2,1,0:T(8,128)(2,1)S(1)}, bf16[3,3,3,256,256]{4,3,2,1,0:T(8,128)(2,1)}, u32[]{:S(2)}) %copy-start.1) | copy-done | bytes 3538968
  4.6 0.0 copy-start.2
  4.6 0.9 %copy-done.2 = bf16[1,2,4,32,256]{4,3,2,1,0:T(8,128)(2,1)S(1)} copy-done((bf16[1,2,4,32,256]{4,3,2,1,0:T(8,128)(2,1)S(1)}, bf16[1,2,4,32,256]{4,3,2,1,0:T(8,128)(2,1)}, u32[]{:S(2)}) %copy-start.2) | copy-done | bytes 131096
  5.5 0.0 copy-start.3
  5.5 0.7 %copy-done.3 = bf16[1,1,2,16,256]{4,3,2,1,0:T(8,128)(2,1)S(1)} copy-done((bf16[1,1,2,16,256]{4,3,2,1,0:T(8,128)(2,1)S(1)}, bf16[1,1,2,16,256]{4,3,2,1,0:T(8,128)(2,1)}, u32[]{:S(2)}) %copy-start.3) | copy-done | bytes 16408
  6.3 58.2 %shard_map.75 = (bf16[32,256]{1,0:T(8,128)(2,1)S(1)}, bf16[256,256]{1,0:T(8,128)(2,1)S(1)}, f32[216,256]{1,0:T(8,128)S(1)}, f32[216,256]{1,0:T(8,128)S(1)}) custom-call(bf16[256,256]{1,0:T(8,128)(2,1)S(1)} %bitcast.8, bf16[27,256,256]{2,1,0:T(8,128)(2,1)S(1)} %bitcast.6, bf16[27,256,256]{2,1,0:T(8,128)(2,1)S(1)} %bitcast.7, bf16[32,256]{1,0:T(8,128)(2,1)S(1)} %bitcast.10), custom_call_target="tpu_custom_call" | custom-call | tf_op jit(solution)/shard_map/pallas_call | solution.py:508
  64.5 0.6 copy.12
  65.1 0.7 copy.13
  65.7 0.7 %copy.14 = f32[216,256]{1,0:T(8,128)} copy(f32[216,256]{1,0:T(8,128)S(1)} %get-tuple-element.18) | data formatting | bytes 442368
  66.4 0.7 %copy.15 = f32[216,256]{1,0:T(8,128)} copy(f32[216,256]{1,0:T(8,128)S(1)} %get-tuple-element.19) | data formatting | bytes 442368
Async XLA Ops:
  0.6 2.0 %copy-start = (bf16[3,3,3,256,256]{4,3,2,1,0:T(8,128)(2,1)S(1)}, bf16[3,3,3,256,256]{4,3,2,1,0:T(8,128)(2,1)}, u32[]{:S(2)}) copy-start(bf16[3,3,3,256,256]{4,3,2,1,0:T(8,128)(2,1)} %param.5) | copy-start | bytes 10616836
  2.6 2.0 %copy-start.1 = (bf16[3,3,3,256,256]{4,3,2,1,0:T(8,128)(2,1)S(1)}, bf16[3,3,3,256,256]{4,3,2,1,0:T(8,128)(2,1)}, u32[]{:S(2)}) copy-start(bf16[3,3,3,256,256]{4,3,2,1,0:T(8,128)(2,1)} %param.6) | copy-start | bytes 10616836
  4.6 0.9 %copy-start.2 = (bf16[1,2,4,32,256]{4,3,2,1,0:T(8,128)(2,1)S(1)}, bf16[1,2,4,32,256]{4,3,2,1,0:T(8,128)(2,1)}, u32[]{:S(2)}) copy-start(bf16[1,2,4,32,256]{4,3,2,1,0:T(8,128)(2,1)} %param.4) | copy-start | bytes 393220
  5.5 0.7 %copy-start.3 = (bf16[1,1,2,16,256]{4,3,2,1,0:T(8,128)(2,1)S(1)}, bf16[1,1,2,16,256]{4,3,2,1,0:T(8,128)(2,1)}, u32[]{:S(2)}) copy-start(bf16[1,1,2,16,256]{4,3,2,1,0:T(8,128)(2,1)} %param.7) | copy-start | bytes 49156

commit v2 on v1

v2 whole, which is shorter than its diff:
```python
import functools
import math

import jax
import jax.numpy as jnp
from jax import lax
from jax.experimental import pallas as pl
from jax.experimental.pallas import tpu as pltpu
from jax.sharding import PartitionSpec as P

MESH = pl.DeviceIdType.MESH
F32 = jnp.float32
BF16 = jnp.bfloat16
NT = (((1,), (1,)), ((), ()))
TN = (((0,), (0,)), ((), ()))


def iota2(shape, dim):
    return lax.broadcasted_iota(jnp.int32, shape, dim)


def one_hot(mask):
    return jnp.where(mask, 1.0, 0.0).astype(F32).astype(BF16)


def column_order(n):
    m, k = iota2((n, n), 0), iota2((n, n), 1)
    return one_hot(k == (m & ~31) + 2 * (m & 15) + ((m >> 4) & 1))


def channel_order(n):
    i, k = iota2((n, n), 0), iota2((n, n), 1)
    j = k & 127
    return one_hot(i == (j >> 3) * 16 + (k >> 7) * 8 + (j & 7))


def quarter_order(n):
    i, k = iota2((2 * n, 2 * n), 0), iota2((2 * n, 2 * n), 1)
    j = k & 63
    return one_hot(i == ((k >> 6) & 1) * n + (j >> 3) * 32 + (k >> 7) * 8 + (j & 7))


def move_in_16(x, step):
    n = x.shape[0]
    k = iota2(x.shape, 0) & 15
    rolled = pltpu.roll(x, step % n, 0)
    return jnp.where(k == (0 if step == 1 else 15), 0.0, rolled)


def halves(x):
    groups = x.shape[0] // 32
    parts = x.reshape(groups, 2, 16, x.shape[1])
    return parts[:, 0].reshape(groups * 16, -1), parts[:, 1].reshape(groups * 16, -1)


def joined(even, odd):
    groups = even.shape[0] // 16
    parts = [h.reshape(groups, 1, 16, h.shape[1]) for h in (even, odd)]
    return jnp.concatenate(parts, axis=1).reshape(groups * 32, -1)


def from_left(x):
    even, odd = halves(x)
    return joined(move_in_16(odd, 1), even)


def from_right(x):
    even, odd = halves(x)
    return joined(odd, move_in_16(even, -1))


def kernel(
    sizes,
    x_hbm, w1_hbm, w2_hbm, og_hbm,
    enc_ref, clip_ref, fg,
    x_ref, og_ref, w1, w2, xe, oge, he, ge, hg, zs,
    xs, xsh, gs, hs, hsh, xg, xgh, gg, hgat, hgh, ogat, xt, g3, part, part4,
    sl, r1, s1, r2, fs,
    wsem, p1s, p1r, p2s, p2r,
    xss, xsr, xhs, xhr, gss, gsr, hss, hsr, hhs, hhr, oss, osr,
    rs1s, rs1r, rs2s, rs2r, ags, agr,
):
    nt, nh, nd = sizes
    ny, nz = 2 * nd, nh // 2
    t, h, d = lax.axis_index("tm"), lax.axis_index("height"), lax.axis_index("dp")
    y, z = (h % 2) * nd + d, h // 2
    core, chip = t % 2, t // 2
    t_next, t_prev = (t + 1) % nt, (t + nt - 1) % nt
    h_next, h_prev = (h + 1) % nh, (h + nh - 1) % nh
    block = z * ny + y
    groups = 864 // (ny * nz)
    slot = 8 * ((groups + 1) // 2)

    wc1 = pltpu.make_async_copy(w1_hbm, w1, wsem.at[0])
    wc2 = pltpu.make_async_copy(w2_hbm, w2, wsem.at[1])
    og_in = pltpu.make_async_copy(og_hbm, og_ref, wsem.at[2])
    x_in = pltpu.make_async_copy(x_hbm, x_ref, wsem.at[3])
    for c in (og_in, x_in, wc2, wc1):
        c.start()

    def at_y(k):
        return (t, z * 2 + k // nd, k % nd)

    barrier = pltpu.get_barrier_semaphore()

    def greet(where):
        pl.semaphore_signal(barrier, inc=1, device_id=where, device_id_type=MESH)

    for k in range(1, nt):
        greet(((t + k) % nt, h, d))
    for hh in (h_next, h_prev):
        for tt in (t_prev, t, t_next):
            greet((tt, hh, d))
    for k in range(1, ny):
        greet(at_y((y + k) % ny))
    for k in range(1, nz):
        greet((t, ((z + k) % nz) * 2 + h % 2, d))

    og_in.wait()
    x_in.wait()
    x_own = jnp.dot(column_order(256), x_ref[...], preferred_element_type=F32).astype(BF16)
    xe[2:4, 1:5] = x_own.reshape(2, 4, 32, 256)
    oge[0, 1:3] = og_ref[...].reshape(2, 16, 256)
    by_channel = channel_order(256)

    def keep_halves(block, out, rows):
        moved = jnp.dot(block, by_channel, preferred_element_type=F32).astype(BF16)
        for k in range(2):
            out[k] = moved[:, 128 * k : 128 * (k + 1)].reshape(2, rows, 32, 128)

    keep_halves(x_own, xs, 4)

    pl.semaphore_wait(barrier, (nt - 1) + 6 + (ny - 1) + (nz - 1))

    def send(src, dst, ssem, rsem, where):
        return pltpu.make_async_remote_copy(
            src_ref=src, dst_ref=dst, send_sem=ssem, recv_sem=rsem, device_id=where, device_id_type=MESH
        )

    def p1(k, src, dst, where):
        return send(src, dst, p1s.at[k], p1r.at[k], where)

    og_halo = [
        p1(0, oge.at[0:1, 1:3], oge.at[1:2, 1:3], (t_prev, h, d)),
        p1(1, oge.at[0:1, 2:3], oge.at[0:1, 0:1], (t, h_next, d)),
        p1(2, oge.at[0:1, 2:3], oge.at[1:2, 0:1], (t_prev, h_next, d)),
    ]
    x_halo = [
        p1(3, xe.at[2:4, 1:5], xe.at[0:2, 1:5], (t_next, h, d)),
        p1(4, xe.at[2:4, 4:5], xe.at[2:4, 0:1], (t, h_next, d)),
        p1(5, xe.at[2:4, 1:2], xe.at[2:4, 5:6], (t, h_prev, d)),
        p1(6, xe.at[2:4, 4:5], xe.at[0:2, 0:1], (t_next, h_next, d)),
        p1(7, xe.at[2:4, 1:2], xe.at[0:2, 5:6], (t_next, h_prev, d)),
    ]
    for c in og_halo + x_halo:
        c.start()

    def gather_sends(role, source, target, ssem, rsem):
        for k in range(nt // 2):
            to_chip = (chip + k) % (nt // 2)
            to = to_chip * 2 + role
            c = send(source(to_chip), target(t), ssem.at[k], rsem.at[t], (to, h, d))
            if k == 0:
                pl.when(core != role)(c.start)
            else:
                c.start()

    def gather_sent(role, source, target, ssem, rsem):
        for k in range(nt // 2):
            to_chip = (chip + k) % (nt // 2)
            c = send(source(to_chip), target(t), ssem.at[k], rsem.at[t], (to_chip * 2 + role, h, d))
            if k == 0:
                pl.when(core != role)(c.wait_send)
            else:
                c.wait_send()

    def gather_received(source, target, ssem, rsem):
        for k in range(1, nt):
            s = (t + k) % nt
            send(source(0), target(s), ssem.at[0], rsem.at[s], (s, h, d)).wait_recv()

    def later_frames(ref):
        return lambda s: ref.at[pl.ds(2 + 2 * s, 2)]

    og_move = (lambda c: oge.at[0, 1:3], lambda s: ogat.at[s], oss, osr)
    x_move = (lambda c: xs.at[c // 2], later_frames(xg), xss, xsr)
    x_rim_move = (lambda c: xsh.at[c // 2], later_frames(xgh), xhs, xhr)
    g_move = (lambda c: gs.at[c % 2], lambda s: gg.at[pl.ds(2 * s, 2)], gss, gsr)
    h_move = (lambda c: hs.at[c], later_frames(hgat), hss, hsr)
    h_rim_move = (lambda c: hsh.at[c], later_frames(hgh), hhs, hhr)
    gather_sends(1, *og_move)

    wc2.wait()
    for c in og_halo:
        c.wait_recv()
    gather_sends(0, *x_move)

    @pl.when(t == nt - 1)
    def _():
        oge[1] = jnp.zeros((3, 16, 256), BF16)

    @pl.when(h == 0)
    def _():
        oge[:, 0] = jnp.zeros((2, 16, 256), BF16)

    og_rows = oge[...].reshape(96, 256)
    first = t == 0
    terms = {}
    for e in range(3):
        for a in range(3):
            for b in range(3):
                lhs = og_rows if a < 2 else og_rows[:48]
                q = lax.dot_general(lhs, w2[a * 9 + b * 3 + e], NT, preferred_element_type=F32)
                offset = 0 if b == 2 else 16
                here = q[offset : offset + 32]
                if a < 2:
                    here = jnp.where(first, here, 0.0)
                    later = q[48 + offset : 48 + offset + 32]
                    key = (a, b % 2, e)
                    terms[key] = terms.get(key, 0.0) + later
                key = (0, b % 2, e)
                terms[key] = terms.get(key, 0.0) + here
    for f in range(2):
        for b in range(2):
            even = terms[f, b, 0] + move_in_16(terms[f, b, 2], 1)
            odd = terms[f, b, 1]
            for u in range(2):
                hg[f, 2 * u + b, 0:16] = even[16 * u : 16 * u + 16]
                hg[f, 2 * u + b, 16:32] = odd[16 * u : 16 * u + 16]

    for c in x_halo:
        c.wait_recv()

    @pl.when(h == 0)
    def _():
        xe[:, 0] = jnp.zeros((4, 32, 256), BF16)

    @pl.when(h == nh - 1)
    def _():
        xe[:, 5] = jnp.zeros((4, 32, 256), BF16)

    @pl.when(first)
    def _():
        xe[0] = xe[2]
        xe[1] = xe[2]

    rims = jnp.concatenate([xe[2:4, 0:1], xe[2:4, 5:6]], axis=1)
    keep_halves(rims.reshape(128, 256), xsh, 2)
    gather_sends(0, *x_rim_move)

    wc1.wait()
    sums = [None] * 3
    for a in range(3):
        for b in range(3):
            lhs = xe[a : a + 2, b : b + 4].reshape(256, 256)
            for e in range(3):
                q = jnp.dot(lhs, w1[a * 9 + b * 3 + e], preferred_element_type=F32)
                sums[e] = q if sums[e] is None else sums[e] + q
    value = from_left(sums[0]) + sums[1] + from_right(sums[2])
    sigmoid = jax.nn.sigmoid(value)
    he[2:4, 0:4] = (value * sigmoid).astype(BF16).reshape(2, 4, 32, 256)
    slope = sigmoid * (1.0 + value * (1.0 - sigmoid))
    grad = (hg[...].reshape(256, 256) * slope).astype(BF16)
    ge[0:2, 1:5] = grad.reshape(2, 4, 32, 256)
    for k in range(2):
        gs[k] = grad[:, 128 * k : 128 * (k + 1)].reshape(2, 4, 32, 128)

    def p2(k, src, dst, where):
        return send(src, dst, p2s.at[k], p2r.at[k], where)

    h_rows = p2(0, he.at[2:4, 0:1], he.at[2:4, 4:5], (t, h_prev, d))
    g_rows = [
        p2(1, ge.at[0:2, 4:5], ge.at[0:2, 0:1], (t, h_next, d)),
        p2(2, ge.at[0:2, 1:2], ge.at[0:2, 5:6], (t, h_prev, d)),
    ]
    h_frames = p2(3, he.at[2:4], he.at[0:2], (t_next, h, d))
    g_frames = p2(4, ge.at[0:2], ge.at[2:4], (t_prev, h, d))
    h_rows.start()
    gather_sends(0, *g_move)
    by_quarter = quarter_order(256)

    def keep_quarters(block, out, rows):
        lanes = [block[..., p : p + 16, :].reshape(32 * rows, 256) for p in (0, 16)]
        both = jnp.concatenate(lanes, axis=1)
        moved = jnp.dot(both, by_quarter, preferred_element_type=F32).astype(BF16)
        for k in range(4):
            out[k] = moved[:, 128 * k : 128 * (k + 1)].reshape(2, rows, 16, 128)

    keep_quarters(he[2:4, 0:4], hs, 4)
    gather_sends(1, *h_move)
    for c in g_rows:
        c.start()
    h_rows.wait_recv()

    @pl.when(h == nh - 1)
    def _():
        he[2:4, 4] = jnp.zeros((2, 32, 256), BF16)

    keep_quarters(he[2:4, 4:5], hsh, 1)
    gather_sends(1, *h_rim_move)
    for c in g_rows:
        c.wait_recv()

    @pl.when(h == 0)
    def _():
        ge[0:2, 0] = jnp.zeros((2, 32, 256), BF16)

    @pl.when(h == nh - 1)
    def _():
        ge[0:2, 5] = jnp.zeros((2, 32, 256), BF16)

    @pl.when(core == 0)
    def _():
        part[pl.ds(27 * 128, 8)] = jnp.zeros((8, 128), F32)
        xg[pl.ds(2 + 2 * t, 2)] = xs[chip // 2]
        xgh[pl.ds(2 + 2 * t, 2)] = xsh[chip // 2]
        gg[pl.ds(2 * t, 2)] = gs[chip % 2]
        gather_received(*x_move)
        gather_received(*x_rim_move)
        for f in range(2):
            xg[f] = xg[2]
            xgh[f] = xgh[2]

        def turn(f, carry):
            rows = jnp.concatenate([xgh[f, 0:1], xg[f], xgh[f, 1:2]], axis=0)
            for b in range(3):
                xt[f, 128 * b : 128 * (b + 1)] = rows[b : b + 4].reshape(128, 128).T
            return carry

        lax.fori_loop(0, 2 * nt + 2, turn, 0)
        gather_received(*g_move)

        def spread(s, carry):
            rows = pl.ds(pl.multiple_of(256 * s, 256), 256)
            g = gg[pl.ds(2 * s, 2)].reshape(256, 128)
            wide = g.astype(F32)
            g3[rows, 0:128] = from_right(wide).astype(BF16)
            g3[rows, 128:256] = g
            g3[rows, 256:384] = from_left(wide).astype(BF16)
            return carry

        lax.fori_loop(0, nt, spread, 0)

    @pl.when(core == 1)
    def _():
        part4[pl.ds(27 * 64, 8)] = jnp.zeros((8, 256), F32)
        hgat[pl.ds(2 + 2 * t, 2)] = hs[chip]
        hgh[pl.ds(2 + 2 * t, 2)] = hsh[chip]
        ogat[t] = oge[0, 1:3]
        gather_received(*og_move)
        og_all = ogat[...].reshape(32 * nt, 256)
        og_two = jnp.concatenate([og_all, move_in_16(og_all.astype(F32), 1).astype(BF16)], axis=1)
        gather_received(*h_move)
        gather_received(*h_rim_move)
        for f in range(2):
            hgat[f] = hgat[2]
            hgh[f] = hgh[2]
        for a in range(3):
            for b in range(3):
                pieces = [
                    hgh[2 * f + a, 0] if b + 2 * r == 4 else hgat[2 * f + a, b + 2 * r]
                    for f in range(nt)
                    for r in range(2)
                ]
                lhs = jnp.concatenate(pieces, axis=0)
                q = lax.dot_general(lhs, og_two, TN, preferred_element_type=F32)
                n = 64 * (a * 9 + b * 3)
                part4[n : n + 64] = q[0:64, 0:256]
                part4[n + 64 : n + 128] = q[64:128, 0:256]
                part4[n + 128 : n + 192] = q[0:64, 256:512]

    h_frames.start()
    g_frames.start()

    pair = nz // 3 if nz == 8 else 0

    def chunk_at(j):
        if j < 3 * pair:
            return 3 * ((z + j // pair) % 3) + j % pair
        return (2, 5)[j - 3 * pair] if pair else (z + 1 + j) % nz

    def y_copies(j):
        c = chunk_at(j)
        return [
            send(
                sl.at[(y + k) % ny, c], r1.at[k - 1, c],
                rs1s.at[j, k - 1], rs1r.at[j, k - 1], at_y((y + k) % ny),
            )
            for k in range(1, ny)
        ]

    def send_chunk(j):
        c = chunk_at(j)

        def cut(k, carry):
            n = groups * (c * ny + k)

            @pl.when(core == 0)
            def _():
                first_row = pl.multiple_of((n + 1 - chip // 2) // 2 * 8, 8)
                sl[k, c] = part[pl.ds(first_row, slot)].astype(BF16)

            @pl.when(core == 1)
            def _():
                first_row = pl.multiple_of((n + 3 - chip) // 4 * 8, 8)
                rows = part4[pl.ds(first_row, slot // 2)]
                stacked = jnp.concatenate([rows[:, :128], rows[:, 128:]], axis=0)
                sl[k, c] = stacked.astype(BF16)

            return carry

        lax.fori_loop(0, ny, cut, 0)
        for copy in y_copies(j):
            copy.start()

    for k in range(3):

        @pl.when(core == 0)
        def _():
            a = (z + k) % 3
            lhs = jnp.concatenate([xt[a + f] for f in range(2 * nt)], axis=1)
            q = jnp.dot(lhs, g3[...], preferred_element_type=F32)
            for b in range(3):
                for e in range(3):
                    n = pl.multiple_of(128 * (a * 9 + b * 3 + e), 128)
                    part[pl.ds(n, 128)] = q[128 * b : 128 * (b + 1), 128 * e : 128 * (e + 1)]

        for j in range(k * pair, (k + 1) * pair):
            send_chunk(j)
    for j in range(3 * pair, nz):
        send_chunk(j)

    def z_copy(j):
        c = chunk_at(j)
        step = (c - z + nz) % nz
        k = jnp.maximum(step - 1, 0)
        where = (t, c * 2 + h % 2, d)
        return step, send(s1.at[c], r2.at[k], rs2s.at[k], rs2r.at[k], where)

    def pass_chunk(j):
        c = chunk_at(j)
        for copy in y_copies(j):
            copy.wait_recv()
        total = sl[y, c].astype(F32)
        for n in range(ny - 1):
            total = total + r1[n, c].astype(F32)
        s1[c] = total.astype(BF16)
        step, copy = z_copy(j)
        pl.when(step > 0)(copy.start)

    for j in range(nz // 4):
        pass_chunk(j)

    h_frames.wait_recv()

    @pl.when(first)
    def _():
        he[0] = he[2]
        he[1] = he[2]

    sums = [None] * 3
    for a in range(3):
        for b in range(3):
            for e in range(3):
                p = 16 * (e % 2)
                lhs = jnp.concatenate([he[a, b, p : p + 16], he[a, b + 2, p : p + 16]], axis=0)
                q = jnp.dot(lhs, w2[a * 9 + b * 3 + e], preferred_element_type=F32)
                sums[e] = q if sums[e] is None else sums[e] + q
    enc_ref[...] = (sums[0] + sums[1] + move_in_16(sums[2], -1)).astype(BF16)
    for j in range(nz // 4, nz // 2):
        pass_chunk(j)

    g_frames.wait_recv()

    @pl.when(t == nt - 1)
    def _():
        ge[2:4] = jnp.zeros((2, 6, 32, 256), BF16)

    sums = [None] * 3
    for a in range(3):
        for b in range(3):
            lhs = ge[2 - a : 4 - a, 2 - b : 6 - b].reshape(256, 256)
            for e in range(3):
                q = lax.dot_general(lhs, w1[a * 9 + b * 3 + e], NT, preferred_element_type=F32)
                sums[e] = q if sums[e] is None else sums[e] + q
    for e in range(3):
        zs[e] = sums[e]

    for j in range(nz // 2, 3 * nz // 4):
        pass_chunk(j)

    @pl.when(first)
    def _():
        for e in range(3):
            total = zs[e, 0:128]
            for a, f in ((0, 0), (0, 1), (1, 0)):
                for b in range(3):
                    lhs = ge[f, 2 - b : 6 - b].reshape(128, 256)
                    total = total + lax.dot_general(
                        lhs, w1[a * 9 + b * 3 + e], NT, preferred_element_type=F32
                    )
            zs[e, 0:128] = total

    clip = (from_right(zs[0]) + zs[1] + from_left(zs[2])).astype(BF16)
    clip_ref[...] = lax.dot_general(
        column_order(256), clip, TN, preferred_element_type=F32
    ).astype(BF16)

    for j in range(3 * nz // 4, nz):
        pass_chunk(j)
    total = s1[z].astype(F32)
    for k in range(1, nz):
        source = ((z - k + nz) % nz * 2 + h % 2, d)
        send(
            s1.at[z], r2.at[k - 1], rs2s.at[k - 1], rs2r.at[k - 1], (t, *source)
        ).wait_recv()
        total = total + r2[k - 1].astype(F32)
    fs[...] = total.astype(BF16)
    t_sends = []
    for k in range(1, nt):
        where = ((t + k) % nt, h, d)
        t_sends.append(send(fs, fg.at[t], ags.at[k - 1], agr.at[k - 1], where))
    for c in t_sends:
        c.start()
    fg[t] = fs[...]
    for k in range(1, nt):
        s = (t + nt - k) % nt
        send(fs, fg.at[s], ags.at[k - 1], agr.at[k - 1], (s, h, d)).wait_recv()

    for c in og_halo + x_halo + [h_rows] + g_rows + [h_frames, g_frames] + t_sends:
        c.wait_send()
    for j in range(nz):
        for copy in y_copies(j):
            copy.wait_send()
        step, copy = z_copy(j)
        pl.when(step > 0)(copy.wait_send)
    for move in (x_move, x_rim_move, g_move):
        gather_sent(0, *move)
    for move in (og_move, h_move, h_rim_move):
        gather_sent(1, *move)


def finish(sizes, enc_ref, clip_ref, fg, enc_hbm, clip_hbm, conv_hbm, down_hbm, ff, conv, down, sem):
    nt, nh, nd = sizes
    block = lax.axis_index("height") * nd + lax.axis_index("dp")
    groups = 864 // (nh * nd)
    slot = fg.shape[1]
    early = [
        pltpu.make_async_copy(enc_ref, enc_hbm, sem.at[0]),
        pltpu.make_async_copy(clip_ref, clip_hbm, sem.at[1]),
    ]
    for c in early:
        c.start()
    cells = nt * nh * nd * 256
    scale = (1.0 / math.sqrt(cells), 1.0 / math.sqrt(cells // 8))
    for s in range(nt):
        ff[s] = fg[s].astype(F32) * scale[s % 2]
    late = []
    for k, (out, hbm) in enumerate(((conv, conv_hbm), (down, down_hbm))):
        for j in range(groups):
            n = groups * block + j
            for o in range(2):
                if k == 0:
                    rows = ff[2 * (2 * (n % 2) + o), 8 * (j // 2) : 8 * (j // 2) + 8]
                else:
                    row = o * (slot // 2) + 8 * (j // 4)
                    rows = ff[2 * (n % 4) + 1, row : row + 8]
                out[8 * j : 8 * j + 8, 128 * o : 128 * o + 128] = rows
        c = pltpu.make_async_copy(out, hbm, sem.at[2 + k])
        c.start()
        late.append(c)
    for c in early + late:
        c.wait()


def body(mesh_sizes, video_clip, conv_weight, down_weight, output_grad):
    nt, nh, nd = mesh_sizes
    ny, nz = 2 * nd, nh // 2
    blocks = ny * nz
    groups = 864 // blocks
    slot = 8 * ((groups + 1) // 2)
    dma = pltpu.SemaphoreType.DMA

    def vm(*shape, dtype=BF16):
        return pltpu.VMEM(shape, dtype)

    scratch = [
        vm(256, 256), vm(32, 256), vm(27, 256, 256), vm(27, 256, 256),
        vm(4, 6, 32, 256), vm(2, 3, 16, 256), vm(4, 5, 32, 256), vm(4, 6, 32, 256),
        vm(2, 4, 32, 256, dtype=F32), vm(3, 256, 256, dtype=F32),
        vm(2, 2, 4, 32, 128), vm(2, 2, 2, 32, 128), vm(2, 2, 4, 32, 128),
        vm(4, 2, 4, 16, 128), vm(4, 2, 1, 16, 128),
        vm(2 * nt + 2, 4, 32, 128), vm(2 * nt + 2, 2, 32, 128), vm(2 * nt, 4, 32, 128),
        vm(2 * nt + 2, 4, 16, 128), vm(2 * nt + 2, 1, 16, 128), vm(nt, 2, 16, 256),
        vm(2 * nt + 2, 384, 128), vm(256 * nt, 384),
        vm(27 * 128 + 8, 128, dtype=F32), vm(27 * 64 + 8, 256, dtype=F32),
        vm(ny, nz, slot, 128), vm(ny - 1, nz, slot, 128),
        vm(nz, slot, 128), vm(nz - 1, slot, 128),
        vm(slot, 128),
        dma((4,)), dma((8,)), dma((8,)), dma((5,)), dma((5,)),
    ]
    scratch += [dma((n,)) for _ in range(6) for n in (nt // 2, nt)]
    scratch += [dma(n) for n in ((nz, ny - 1),) * 2 + ((nz - 1,),) * 2 + ((nt - 1,),) * 2]
    vmem = pl.BlockSpec(memory_space=pltpu.VMEM)
    hbm = pl.BlockSpec(memory_space=pltpu.HBM)
    shape = jax.ShapeDtypeStruct
    features = (shape((32, 256), BF16), shape((256, 256), BF16))
    gathered = pl.pallas_call(
        functools.partial(kernel, mesh_sizes),
        out_shape=(*features, shape((nt, slot, 128), BF16)),
        in_specs=[hbm] * 4,
        out_specs=(vmem,) * 3,
        scratch_shapes=scratch,
        compiler_params=pltpu.CompilerParams(
            collective_id=0, has_side_effects=True, vmem_limit_bytes=44 * 2**20
        ),
    )(
        *(
            pltpu.with_memory_space_constraint(operand, pltpu.HBM)
            for operand in (
                video_clip.reshape(256, 256),
                conv_weight.reshape(27, 256, 256),
                down_weight.reshape(27, 256, 256),
                output_grad.reshape(32, 256),
            )
        )
    )
    rows = shape((groups * 8, 256), F32)
    enc, clip, conv, down = pl.pallas_call(
        functools.partial(finish, mesh_sizes),
        out_shape=(*features, rows, rows),
        in_specs=[vmem] * 3,
        out_specs=(hbm,) * 4,
        scratch_shapes=[
            vm(nt, slot, 128, dtype=F32),
            vm(groups * 8, 256, dtype=F32),
            vm(groups * 8, 256, dtype=F32),
            dma((4,)),
        ],
        compiler_params=pltpu.CompilerParams(vmem_limit_bytes=16 * 2**20),
    )(*gathered)
    return enc.reshape(1, 1, 2, 16, 256), clip.reshape(1, 2, 4, 32, 256), conv, down


def solution(mesh):
    sizes = tuple(mesh.shape[a] for a in ("tm", "height", "dp"))
    cells = P("dp", "tm", "height", None, None)
    rows = P(("height", "dp"), None)
    return jax.shard_map(
        functools.partial(body, sizes),
        mesh=mesh,
        in_specs=(cells, P(), P(), cells),
        out_specs=(cells, cells, rows, rows),
        check_vma=False,
    )
```

time: 67.3 us -> 49.7 us (0.74)
  Pallas kernels: 58.2 us -> 48.9 us
  local copies, waits for them, and re-layouts: 8.25 us -> 0 us
    pallas_call x1 -> x2, Pallas kernels: 58.2 us -> 48.9 us  [the longest x1 48 us: body(): pl.pallas_call(functools.partial(kernel, mesh_sizes), out_shape=(*feature...]
    unnamed x12 -> x0, local copies, waits for them, and re-layouts: 8.25 us -> none
where the time goes in v2:
time: 49.7 us; the launch traced here: 49.5 us
  Pallas kernels  48.9 us (98%)
  between operations  0.64 us (1%)
    pallas_call x1, Pallas kernels, body(): pl.pallas_call(functools.partial(kernel, mesh_sizes), out_shape=(*feature...  48 us

profile of v2, /device:TPU:1, one launch (start us, length us, event | category | flops | bytes accessed | tf_op | source)
XLA Modules:
  0.0 49.5 jit_solution(4217683622007827895)
XLA Ops:
  0.6 48.0 %shard_map.75 = (bf16[32,256]{1,0:T(8,128)(2,1)S(1)}, bf16[256,256]{1,0:T(8,128)(2,1)S(1)}, bf16[8,112,128]{2,1,0:T(8,128)(2,1)S(1)}) custom-call(bf16[256,256]{1,0:T(8,128)(2,1)} %bitcast.8, bf16[27,256,256]{2,1,0:T(8,128)(2,1)} %bitcast.6, bf16[27,256,256]{2,1,0:T(8,128)(2,1)} %bitcast.7, bf16[32,256]{1,0:T(8,128)(2,1)} %bitcast.9), custom_call_target="tpu_custom_call" | custom-call | tf_op jit(solution)/shard_map/pallas_call | solution.py:608
  48.6 0.9 %shard_map.76 = (bf16[32,256]{1,0:T(8,128)(2,1)}, bf16[256,256]{1,0:T(8,128)(2,1)}, f32[216,256]{1,0:T(8,128)}, f32[216,256]{1,0:T(8,128)}) custom-call(bf16[32,256]{1,0:T(8,128)(2,1)S(1)} %get-tuple-element.11.enc_ref, bf16[256,256]{1,0:T(8,128)(2,1)S(1)} %get-tuple-element.12.clip_ref, bf16[8,112,128]{2,1,0:T(8,128)(2,1)S(1)} %get-tuple-element.13.fg), custom_call_target="tpu_custom_call" | custom-call | tf_op jit(solution)/shard_map/pallas_call | solution.py:629

commit v3 on v2

--- a/solution.py
+++ b/solution.py
@@ -73,7 +73,7 @@
     sizes,
     x_hbm, w1_hbm, w2_hbm, og_hbm,
     enc_ref, clip_ref, fg,
-    x_ref, og_ref, w1, w2, xe, oge, he, ge, hg, zs,
+    by_column, by_channel, by_quarter, x_ref, og_ref, w1, w2, xe, oge, he, ge, hg, zs,
     xs, xsh, gs, hs, hsh, xg, xgh, gg, hgat, hgh, ogat, xt, g3, part, part4,
     sl, r1, s1, r2, fs,
     wsem, p1s, p1r, p2s, p2r,
@@ -93,9 +93,10 @@
 
     wc1 = pltpu.make_async_copy(w1_hbm, w1, wsem.at[0])
     wc2 = pltpu.make_async_copy(w2_hbm, w2, wsem.at[1])
+    first = t == 0
     og_in = pltpu.make_async_copy(og_hbm, og_ref, wsem.at[2])
     x_in = pltpu.make_async_copy(x_hbm, x_ref, wsem.at[3])
-    for c in (og_in, x_in, wc2, wc1):
+    for c in (x_in, og_in, wc1, wc2):
         c.start()
 
     def at_y(k):
@@ -111,26 +112,33 @@
     for hh in (h_next, h_prev):
         for tt in (t_prev, t, t_next):
             greet((tt, hh, d))
+    for k in range(nt // 2):
+        greet((2 * k + 1, h_prev, d))
+
+    @pl.when(core == 1)
+    def _():
+        for k in range(nt):
+            greet((k, h_next, d))
+
     for k in range(1, ny):
         greet(at_y((y + k) % ny))
     for k in range(1, nz):
         greet((t, ((z + k) % nz) * 2 + h % 2, d))
 
+    by_column[...] = column_order(256)
     og_in.wait()
     x_in.wait()
-    x_own = jnp.dot(column_order(256), x_ref[...], preferred_element_type=F32).astype(BF16)
+    x_own = jnp.dot(by_column[...], x_ref[...], preferred_element_type=F32).astype(BF16)
     xe[2:4, 1:5] = x_own.reshape(2, 4, 32, 256)
     oge[0, 1:3] = og_ref[...].reshape(2, 16, 256)
-    by_channel = channel_order(256)
 
     def keep_halves(block, out, rows):
-        moved = jnp.dot(block, by_channel, preferred_element_type=F32).astype(BF16)
+        moved = jnp.dot(block, by_channel[...], preferred_element_type=F32).astype(BF16)
         for k in range(2):
             out[k] = moved[:, 128 * k : 128 * (k + 1)].reshape(2, rows, 32, 128)
 
-    keep_halves(x_own, xs, 4)
-
-    pl.semaphore_wait(barrier, (nt - 1) + 6 + (ny - 1) + (nz - 1))
+    greetings = (nt - 1) + 6 + (ny - 1) + (nz - 1) + nt // 2
+    pl.semaphore_wait(barrier, greetings + core * nt)
 
     def send(src, dst, ssem, rsem, where):
         return pltpu.make_async_remote_copy(
@@ -155,29 +163,35 @@
     for c in og_halo + x_halo:
         c.start()
 
-    def gather_sends(role, source, target, ssem, rsem):
+    def gather_sends(role, source, target, ssem, rsem, to_h=None):
+        rim = to_h is not None
+        to_h = to_h if rim else h
         for k in range(nt // 2):
             to_chip = (chip + k) % (nt // 2)
             to = to_chip * 2 + role
-            c = send(source(to_chip), target(t), ssem.at[k], rsem.at[t], (to, h, d))
-            if k == 0:
+            c = send(source(to_chip), target(t), ssem.at[k], rsem.at[t], (to, to_h, d))
+            if k == 0 and not rim:
                 pl.when(core != role)(c.start)
             else:
                 c.start()
 
-    def gather_sent(role, source, target, ssem, rsem):
+    def gather_sent(role, source, target, ssem, rsem, to_h=None):
+        rim = to_h is not None
+        to_h = to_h if rim else h
         for k in range(nt // 2):
             to_chip = (chip + k) % (nt // 2)
-            c = send(source(to_chip), target(t), ssem.at[k], rsem.at[t], (to_chip * 2 + role, h, d))
-            if k == 0:
+            to = to_chip * 2 + role
+            c = send(source(to_chip), target(t), ssem.at[k], rsem.at[t], (to, to_h, d))
+            if k == 0 and not rim:
                 pl.when(core != role)(c.wait_send)
             else:
                 c.wait_send()
 
-    def gather_received(source, target, ssem, rsem):
-        for k in range(1, nt):
+    def gather_received(source, target, ssem, rsem, from_h=None):
+        for k in range(0 if from_h is not None else 1, nt):
             s = (t + k) % nt
-            send(source(0), target(s), ssem.at[0], rsem.at[s], (s, h, d)).wait_recv()
+            where = (s, h if from_h is None else from_h, d)
+            send(source(0), target(s), ssem.at[0], rsem.at[s], where).wait_recv()
 
     def later_frames(ref):
         return lambda s: ref.at[pl.ds(2 + 2 * s, 2)]
@@ -190,44 +204,14 @@
     h_rim_move = (lambda c: hsh.at[c], later_frames(hgh), hhs, hhr)
     gather_sends(1, *og_move)
 
-    wc2.wait()
+    by_channel[...] = channel_order(256)
+    keep_halves(x_own, xs, 4)
+    by_quarter[...] = quarter_order(256)
+    part[pl.ds(27 * 128, 8)] = jnp.zeros((8, 128), F32)
+    part4[pl.ds(27 * 64, 8)] = jnp.zeros((8, 256), F32)
     for c in og_halo:
         c.wait_recv()
     gather_sends(0, *x_move)
-
-    @pl.when(t == nt - 1)
-    def _():
-        oge[1] = jnp.zeros((3, 16, 256), BF16)
-
-    @pl.when(h == 0)
-    def _():
-        oge[:, 0] = jnp.zeros((2, 16, 256), BF16)
-
-    og_rows = oge[...].reshape(96, 256)
-    first = t == 0
-    terms = {}
-    for e in range(3):
-        for a in range(3):
-            for b in range(3):
-                lhs = og_rows if a < 2 else og_rows[:48]
-                q = lax.dot_general(lhs, w2[a * 9 + b * 3 + e], NT, preferred_element_type=F32)
-                offset = 0 if b == 2 else 16
-                here = q[offset : offset + 32]
-                if a < 2:
-                    here = jnp.where(first, here, 0.0)
-                    later = q[48 + offset : 48 + offset + 32]
-                    key = (a, b % 2, e)
-                    terms[key] = terms.get(key, 0.0) + later
-                key = (0, b % 2, e)
-                terms[key] = terms.get(key, 0.0) + here
-    for f in range(2):
-        for b in range(2):
-            even = terms[f, b, 0] + move_in_16(terms[f, b, 2], 1)
-            odd = terms[f, b, 1]
-            for u in range(2):
-                hg[f, 2 * u + b, 0:16] = even[16 * u : 16 * u + 16]
-                hg[f, 2 * u + b, 16:32] = odd[16 * u : 16 * u + 16]
-
     for c in x_halo:
         c.wait_recv()
 
@@ -259,11 +243,7 @@
     value = from_left(sums[0]) + sums[1] + from_right(sums[2])
     sigmoid = jax.nn.sigmoid(value)
     he[2:4, 0:4] = (value * sigmoid).astype(BF16).reshape(2, 4, 32, 256)
-    slope = sigmoid * (1.0 + value * (1.0 - sigmoid))
-    grad = (hg[...].reshape(256, 256) * slope).astype(BF16)
-    ge[0:2, 1:5] = grad.reshape(2, 4, 32, 256)
-    for k in range(2):
-        gs[k] = grad[:, 128 * k : 128 * (k + 1)].reshape(2, 4, 32, 128)
+    zs[0] = sigmoid * (1.0 + value * (1.0 - sigmoid))
 
     def p2(k, src, dst, where):
         return send(src, dst, p2s.at[k], p2r.at[k], where)
@@ -275,43 +255,68 @@
     ]
     h_frames = p2(3, he.at[2:4], he.at[0:2], (t_next, h, d))
     g_frames = p2(4, ge.at[0:2], ge.at[2:4], (t_prev, h, d))
-    h_rows.start()
-    gather_sends(0, *g_move)
-    by_quarter = quarter_order(256)
-
     def keep_quarters(block, out, rows):
         lanes = [block[..., p : p + 16, :].reshape(32 * rows, 256) for p in (0, 16)]
         both = jnp.concatenate(lanes, axis=1)
-        moved = jnp.dot(both, by_quarter, preferred_element_type=F32).astype(BF16)
+        moved = jnp.dot(both, by_quarter[...], preferred_element_type=F32).astype(BF16)
         for k in range(4):
             out[k] = moved[:, 128 * k : 128 * (k + 1)].reshape(2, rows, 16, 128)
 
     keep_quarters(he[2:4, 0:4], hs, 4)
+    for k in range(4):
+        hsh[k] = hs[k, :, 0:1]
+    gather_sends(1, *h_rim_move, h_prev)
     gather_sends(1, *h_move)
+    h_rows.start()
+
+    wc2.wait()
+
+    @pl.when(t == nt - 1)
+    def _():
+        oge[1] = jnp.zeros((3, 16, 256), BF16)
+
+    @pl.when(h == 0)
+    def _():
+        oge[:, 0] = jnp.zeros((2, 16, 256), BF16)
+
+    og_rows = oge[...].reshape(96, 256)
+
+    def spread_og(a, b, e):
+        lhs = og_rows if a < 2 else og_rows[:48]
+        q = lax.dot_general(lhs, w2[a * 9 + b * 3 + e], NT, preferred_element_type=F32)
+        offset = 0 if b == 2 else 16
+        here, later = q[offset : offset + 32], q[48 + offset : 48 + offset + 32]
+        return (jnp.where(first, here, 0.0), later) if a < 2 else (here, None)
+
+    early = {}
+    for f in (1, 0):
+        terms = dict(early)
+        for a in (1,) if f else (0, 2):
+            for b in range(3):
+                for e in range(3):
+                    key = (b % 2, e)
+                    here, later = spread_og(a, b, e)
+                    if f:
+                        early[key] = early.get(key, 0.0) + here
+                        terms[key] = terms.get(key, 0.0) + later
+                    else:
+                        terms[key] = terms[key] + (here if a else here + later)
+        for b in range(2):
+            even = terms[b, 0] + move_in_16(terms[b, 2], 1)
+            odd = terms[b, 1]
+            for u in range(2):
+                hg[f, 2 * u + b, 0:16] = even[16 * u : 16 * u + 16]
+                hg[f, 2 * u + b, 16:32] = odd[16 * u : 16 * u + 16]
+        grad = (hg[f].reshape(128, 256) * zs[0, 128 * f : 128 * f + 128]).astype(BF16)
+        ge[f, 1:5] = grad.reshape(4, 32, 256)
+        for k in range(2):
+            gs[k, f] = grad[:, 128 * k : 128 * (k + 1)].reshape(4, 32, 128)
+    gather_sends(0, *g_move)
     for c in g_rows:
         c.start()
-    h_rows.wait_recv()
-
-    @pl.when(h == nh - 1)
-    def _():
-        he[2:4, 4] = jnp.zeros((2, 32, 256), BF16)
-
-    keep_quarters(he[2:4, 4:5], hsh, 1)
-    gather_sends(1, *h_rim_move)
-    for c in g_rows:
-        c.wait_recv()
-
-    @pl.when(h == 0)
-    def _():
-        ge[0:2, 0] = jnp.zeros((2, 32, 256), BF16)
-
-    @pl.when(h == nh - 1)
-    def _():
-        ge[0:2, 5] = jnp.zeros((2, 32, 256), BF16)
 
     @pl.when(core == 0)
     def _():
-        part[pl.ds(27 * 128, 8)] = jnp.zeros((8, 128), F32)
         xg[pl.ds(2 + 2 * t, 2)] = xs[chip // 2]
         xgh[pl.ds(2 + 2 * t, 2)] = xsh[chip // 2]
         gg[pl.ds(2 * t, 2)] = gs[chip % 2]
@@ -343,15 +348,18 @@
 
     @pl.when(core == 1)
     def _():
-        part4[pl.ds(27 * 64, 8)] = jnp.zeros((8, 256), F32)
         hgat[pl.ds(2 + 2 * t, 2)] = hs[chip]
-        hgh[pl.ds(2 + 2 * t, 2)] = hsh[chip]
         ogat[t] = oge[0, 1:3]
         gather_received(*og_move)
         og_all = ogat[...].reshape(32 * nt, 256)
         og_two = jnp.concatenate([og_all, move_in_16(og_all.astype(F32), 1).astype(BF16)], axis=1)
         gather_received(*h_move)
-        gather_received(*h_rim_move)
+        gather_received(*h_rim_move, h_next)
+
+        @pl.when(h == nh - 1)
+        def _():
+            hgh[...] = jnp.zeros(hgh.shape, BF16)
+
         for f in range(2):
             hgat[f] = hgat[2]
             hgh[f] = hgh[2]
@@ -369,55 +377,64 @@
                 part4[n + 64 : n + 128] = q[64:128, 0:256]
                 part4[n + 128 : n + 192] = q[0:64, 256:512]
 
-    h_frames.start()
-    g_frames.start()
-
-    pair = nz // 3 if nz == 8 else 0
+    def coded(codes):
+        code = codes[0]
+        for k in range(1, nz):
+            code = jnp.where(z == k, codes[k], code)
+        return code
+
+    chunk_code = coded(
+        (0o1276534, 0o10276534, 0o21034576, 0o32451067,
+         0o43526710, 0o56743201, 0o67543201, 0o76501243)
+    )
+    tap_code = coded((0o21, 0o21, 0o12, 0o102, 0o120, 0o210, 0o210, 0o201))
 
     def chunk_at(j):
-        if j < 3 * pair:
-            return 3 * ((z + j // pair) % 3) + j % pair
-        return (2, 5)[j - 3 * pair] if pair else (z + 1 + j) % nz
-
-    def y_copies(j):
-        c = chunk_at(j)
+        return chunk_code // 8**j % 8
+
+    def tap_at(j):
+        return tap_code // 8**j % 8
+
+    def y_copies(i):
+        two = pl.ds(2 * i, 2)
         return [
             send(
-                sl.at[(y + k) % ny, c], r1.at[k - 1, c],
-                rs1s.at[j, k - 1], rs1r.at[j, k - 1], at_y((y + k) % ny),
+                sl.at[(y + k) % ny, two], r1.at[k - 1, two],
+                rs1s.at[i, k - 1], rs1r.at[i, k - 1], at_y((y + k) % ny),
             )
-            for k in range(1, ny)
+            for k in (2, 1, 3)
         ]
 
-    def send_chunk(j):
-        c = chunk_at(j)
-
-        def cut(k, carry):
+    def send_chunks(i):
+        def cut(m, carry):
+            j, k = 2 * i + m // ny, m % ny
+            c = chunk_at(j)
             n = groups * (c * ny + k)
 
             @pl.when(core == 0)
             def _():
                 first_row = pl.multiple_of((n + 1 - chip // 2) // 2 * 8, 8)
-                sl[k, c] = part[pl.ds(first_row, slot)].astype(BF16)
+                sl[k, j] = part[pl.ds(first_row, slot)].astype(BF16)
 
             @pl.when(core == 1)
             def _():
                 first_row = pl.multiple_of((n + 3 - chip) // 4 * 8, 8)
                 rows = part4[pl.ds(first_row, slot // 2)]
                 stacked = jnp.concatenate([rows[:, :128], rows[:, 128:]], axis=0)
-                sl[k, c] = stacked.astype(BF16)
+                sl[k, j] = stacked.astype(BF16)
 
             return carry
 
-        lax.fori_loop(0, ny, cut, 0)
-        for copy in y_copies(j):
+        lax.fori_loop(0, 2 * ny, cut, 0)
+        for copy in y_copies(i):
             copy.start()
+
 
     for k in range(3):
 
         @pl.when(core == 0)
         def _():
-            a = (z + k) % 3
+            a = tap_at(k)
             lhs = jnp.concatenate([xt[a + f] for f in range(2 * nt)], axis=1)
             q = jnp.dot(lhs, g3[...], preferred_element_type=F32)
             for b in range(3):
@@ -425,31 +442,41 @@
                     n = pl.multiple_of(128 * (a * 9 + b * 3 + e), 128)
                     part[pl.ds(n, 128)] = q[128 * b : 128 * (b + 1), 128 * e : 128 * (e + 1)]
 
-        for j in range(k * pair, (k + 1) * pair):
-            send_chunk(j)
-    for j in range(3 * pair, nz):
-        send_chunk(j)
+        send_chunks(k)
+    send_chunks(3)
+    h_rows.wait_recv()
+    for c in g_rows:
+        c.wait_recv()
+
+    @pl.when(h == 0)
+    def _():
+        ge[0:2, 0] = jnp.zeros((2, 32, 256), BF16)
+
+    @pl.when(h == nh - 1)
+    def _():
+        he[2:4, 4] = jnp.zeros((2, 32, 256), BF16)
+        ge[0:2, 5] = jnp.zeros((2, 32, 256), BF16)
+
+    h_frames.start()
+    g_frames.start()
+
 
     def z_copy(j):
         c = chunk_at(j)
-        step = (c - z + nz) % nz
-        k = jnp.maximum(step - 1, 0)
+        k = (c - z + nz) % nz - 1
         where = (t, c * 2 + h % 2, d)
-        return step, send(s1.at[c], r2.at[k], rs2s.at[k], rs2r.at[k], where)
-
-    def pass_chunk(j):
-        c = chunk_at(j)
-        for copy in y_copies(j):
+        return send(s1.at[c], r2.at[k], rs2s.at[k], rs2r.at[k], where)
+
+    def pass_chunks(i):
+        for copy in y_copies(i):
             copy.wait_recv()
-        total = sl[y, c].astype(F32)
-        for n in range(ny - 1):
-            total = total + r1[n, c].astype(F32)
-        s1[c] = total.astype(BF16)
-        step, copy = z_copy(j)
-        pl.when(step > 0)(copy.start)
-
-    for j in range(nz // 4):
-        pass_chunk(j)
+        for j in (2 * i, 2 * i + 1):
+            total = sl[y, j].astype(F32)
+            for n in range(ny - 1):
+                total = total + r1[n, j].astype(F32)
+            s1[chunk_at(j)] = total.astype(BF16)
+            if j < nz - 1:
+                z_copy(j).start()
 
     h_frames.wait_recv()
 
@@ -467,8 +494,11 @@
                 q = jnp.dot(lhs, w2[a * 9 + b * 3 + e], preferred_element_type=F32)
                 sums[e] = q if sums[e] is None else sums[e] + q
     enc_ref[...] = (sums[0] + sums[1] + move_in_16(sums[2], -1)).astype(BF16)
-    for j in range(nz // 4, nz // 2):
-        pass_chunk(j)
+    pass_chunks(0)
+    pass_chunks(1)
+
+    pass_chunks(2)
+    pass_chunks(3)
 
     g_frames.wait_recv()
 
@@ -486,9 +516,6 @@
     for e in range(3):
         zs[e] = sums[e]
 
-    for j in range(nz // 2, 3 * nz // 4):
-        pass_chunk(j)
-
     @pl.when(first)
     def _():
         for e in range(3):
@@ -503,11 +530,9 @@
 
     clip = (from_right(zs[0]) + zs[1] + from_left(zs[2])).astype(BF16)
     clip_ref[...] = lax.dot_general(
-        column_order(256), clip, TN, preferred_element_type=F32
+        by_column[...], clip, TN, preferred_element_type=F32
     ).astype(BF16)
 
-    for j in range(3 * nz // 4, nz):
-        pass_chunk(j)
     total = s1[z].astype(F32)
     for k in range(1, nz):
         source = ((z - k + nz) % nz * 2 + h % 2, d)
@@ -529,15 +554,16 @@
 
     for c in og_halo + x_halo + [h_rows] + g_rows + [h_frames, g_frames] + t_sends:
         c.wait_send()
-    for j in range(nz):
-        for copy in y_copies(j):
+    for i in range(nz // 2):
+        for copy in y_copies(i):
             copy.wait_send()
-        step, copy = z_copy(j)
-        pl.when(step > 0)(copy.wait_send)
+    for j in range(nz - 1):
+        z_copy(j).wait_send()
     for move in (x_move, x_rim_move, g_move):
         gather_sent(0, *move)
-    for move in (og_move, h_move, h_rim_move):
+    for move in (og_move, h_move):
         gather_sent(1, *move)
+    gather_sent(1, *h_rim_move, h_prev)
 
 
 def finish(sizes, enc_ref, clip_ref, fg, enc_hbm, clip_hbm, conv_hbm, down_hbm, ff, conv, down, sem):
@@ -585,7 +611,7 @@
         return pltpu.VMEM(shape, dtype)
 
     scratch = [
-        vm(256, 256), vm(32, 256), vm(27, 256, 256), vm(27, 256, 256),
+        vm(256, 256), vm(256, 256), vm(512, 512), vm(256, 256), vm(32, 256), vm(27, 256, 256), vm(27, 256, 256),
         vm(4, 6, 32, 256), vm(2, 3, 16, 256), vm(4, 5, 32, 256), vm(4, 6, 32, 256),
         vm(2, 4, 32, 256, dtype=F32), vm(3, 256, 256, dtype=F32),
         vm(2, 2, 4, 32, 128), vm(2, 2, 2, 32, 128), vm(2, 2, 4, 32, 128),
@@ -600,7 +626,7 @@
         dma((4,)), dma((8,)), dma((8,)), dma((5,)), dma((5,)),
     ]
     scratch += [dma((n,)) for _ in range(6) for n in (nt // 2, nt)]
-    scratch += [dma(n) for n in ((nz, ny - 1),) * 2 + ((nz - 1,),) * 2 + ((nt - 1,),) * 2]
+    scratch += [dma(n) for n in ((nz // 2, ny - 1),) * 2 + ((nz - 1,),) * 2 + ((nt - 1,),) * 2]
     vmem = pl.BlockSpec(memory_space=pltpu.VMEM)
     hbm = pl.BlockSpec(memory_space=pltpu.HBM)
     shape = jax.ShapeDtypeStruct

time: 49.7 us -> 48.4 us (0.974)
  Pallas kernels: 48.9 us -> 47.7 us
    pallas_call x1, Pallas kernels: 48 us -> 46.8 us  [body(): pl.pallas_call(functools.partial(kernel, mesh_sizes), out_shape=(*feature...]
where the time goes in v3:
time: 48.4 us; the launch traced here: 48.3 us
  Pallas kernels  47.7 us (99%)
  between operations  0.64 us (1%)
    pallas_call x1, Pallas kernels, body(): pl.pallas_call(functools.partial(kernel, mesh_sizes), out_shape=(*feature...  46.8 us

profile of v3, /device:TPU:1, one launch (start us, length us, event | category | flops | bytes accessed | tf_op | source)
XLA Modules:
  0.0 48.3 jit_solution(69868229233015389)
XLA Ops:
  0.6 46.8 %shard_map.75 = (bf16[32,256]{1,0:T(8,128)(2,1)S(1)}, bf16[256,256]{1,0:T(8,128)(2,1)S(1)}, bf16[8,112,128]{2,1,0:T(8,128)(2,1)S(1)}) custom-call(bf16[256,256]{1,0:T(8,128)(2,1)} %bitcast.8, bf16[27,256,256]{2,1,0:T(8,128)(2,1)} %bitcast.6, bf16[27,256,256]{2,1,0:T(8,128)(2,1)} %bitcast.7, bf16[32,256]{1,0:T(8,128)(2,1)} %bitcast.9), custom_call_target="tpu_custom_call" | custom-call | tf_op jit(solution)/shard_map/pallas_call | solution.py:634
  47.4 0.9 %shard_map.76 = (bf16[32,256]{1,0:T(8,128)(2,1)}, bf16[256,256]{1,0:T(8,128)(2,1)}, f32[216,256]{1,0:T(8,128)}, f32[216,256]{1,0:T(8,128)}) custom-call(bf16[32,256]{1,0:T(8,128)(2,1)S(1)} %get-tuple-element.11.enc_ref, bf16[256,256]{1,0:T(8,128)(2,1)S(1)} %get-tuple-element.12.clip_ref, bf16[8,112,128]{2,1,0:T(8,128)(2,1)S(1)} %get-tuple-element.13.fg), custom_call_target="tpu_custom_call" | custom-call | tf_op jit(solution)/shard_map/pallas_call | solution.py:655

commit v4 on v3

--- a/solution.py
+++ b/solution.py
@@ -75,10 +75,10 @@
     enc_ref, clip_ref, fg,
     by_column, by_channel, by_quarter, x_ref, og_ref, w1, w2, xe, oge, he, ge, hg, zs,
     xs, xsh, gs, hs, hsh, xg, xgh, gg, hgat, hgh, ogat, xt, g3, part, part4,
-    sl, r1, s1, r2, fs,
+    sl, r1, s1, r2, q1, q2, q3, fs,
     wsem, p1s, p1r, p2s, p2r,
     xss, xsr, xhs, xhr, gss, gsr, hss, hsr, hhs, hhr, oss, osr,
-    rs1s, rs1r, rs2s, rs2r, ags, agr,
+    rs1s, rs1r, rs2s, rs2r, q1s, q1r, q2s, q2r, ags, agr,
 ):
     nt, nh, nd = sizes
     ny, nz = 2 * nd, nh // 2
@@ -96,7 +96,7 @@
     first = t == 0
     og_in = pltpu.make_async_copy(og_hbm, og_ref, wsem.at[2])
     x_in = pltpu.make_async_copy(x_hbm, x_ref, wsem.at[3])
-    for c in (x_in, og_in, wc1, wc2):
+    for c in (x_in, og_in, wc2, wc1):
         c.start()
 
     def at_y(k):
@@ -109,14 +109,19 @@
 
     for k in range(1, nt):
         greet(((t + k) % nt, h, d))
-    for hh in (h_next, h_prev):
-        for tt in (t_prev, t, t_next):
-            greet((tt, hh, d))
     for k in range(nt // 2):
         greet((2 * k + 1, h_prev, d))
 
+    @pl.when(core == 0)
+    def _():
+        greet((t, h_prev, d))
+        for k in (t_prev, t, t_next):
+            greet((k, h_next, d))
+
     @pl.when(core == 1)
     def _():
+        greet((t_prev, h_prev, d))
+        greet((t_next, h_prev, d))
         for k in range(nt):
             greet((k, h_next, d))
 
@@ -137,8 +142,8 @@
         for k in range(2):
             out[k] = moved[:, 128 * k : 128 * (k + 1)].reshape(2, rows, 32, 128)
 
-    greetings = (nt - 1) + 6 + (ny - 1) + (nz - 1) + nt // 2
-    pl.semaphore_wait(barrier, greetings + core * nt)
+    greetings = (nt - 1) + (ny - 1) + (nz - 1) + nt // 2 + 4
+    pl.semaphore_wait(barrier, greetings + core * (nt - 2))
 
     def send(src, dst, ssem, rsem, where):
         return pltpu.make_async_remote_copy(
@@ -212,6 +217,41 @@
     for c in og_halo:
         c.wait_recv()
     gather_sends(0, *x_move)
+
+    wc2.wait()
+
+    @pl.when(t == nt - 1)
+    def _():
+        oge[1] = jnp.zeros((3, 16, 256), BF16)
+
+    @pl.when(h == 0)
+    def _():
+        oge[:, 0] = jnp.zeros((2, 16, 256), BF16)
+
+    og_rows = oge[...].reshape(96, 256)
+    terms = {}
+    for e in range(3):
+        for a in range(3):
+            for b in range(3):
+                lhs = og_rows if a < 2 else og_rows[:48]
+                q = lax.dot_general(lhs, w2[a * 9 + b * 3 + e], NT, preferred_element_type=F32)
+                offset = 0 if b == 2 else 16
+                here = q[offset : offset + 32]
+                if a < 2:
+                    here = jnp.where(first, here, 0.0)
+                    later = q[48 + offset : 48 + offset + 32]
+                    key = (a, b % 2, e)
+                    terms[key] = terms.get(key, 0.0) + later
+                key = (0, b % 2, e)
+                terms[key] = terms.get(key, 0.0) + here
+    for f in range(2):
+        for b in range(2):
+            even = terms[f, b, 0] + move_in_16(terms[f, b, 2], 1)
+            odd = terms[f, b, 1]
+            for u in range(2):
+                hg[f, 2 * u + b, 0:16] = even[16 * u : 16 * u + 16]
+                hg[f, 2 * u + b, 16:32] = odd[16 * u : 16 * u + 16]
+
     for c in x_halo:
         c.wait_recv()
 
@@ -262,56 +302,18 @@
         for k in range(4):
             out[k] = moved[:, 128 * k : 128 * (k + 1)].reshape(2, rows, 16, 128)
 
+    for f in (1, 0):
+        grad = (hg[f].reshape(128, 256) * zs[0, 128 * f : 128 * f + 128]).astype(BF16)
+        ge[f, 1:5] = grad.reshape(4, 32, 256)
+        for k in range(2):
+            gs[k, f] = grad[:, 128 * k : 128 * (k + 1)].reshape(4, 32, 128)
+    gather_sends(0, *g_move)
     keep_quarters(he[2:4, 0:4], hs, 4)
     for k in range(4):
         hsh[k] = hs[k, :, 0:1]
     gather_sends(1, *h_rim_move, h_prev)
     gather_sends(1, *h_move)
     h_rows.start()
-
-    wc2.wait()
-
-    @pl.when(t == nt - 1)
-    def _():
-        oge[1] = jnp.zeros((3, 16, 256), BF16)
-
-    @pl.when(h == 0)
-    def _():
-        oge[:, 0] = jnp.zeros((2, 16, 256), BF16)
-
-    og_rows = oge[...].reshape(96, 256)
-
-    def spread_og(a, b, e):
-        lhs = og_rows if a < 2 else og_rows[:48]
-        q = lax.dot_general(lhs, w2[a * 9 + b * 3 + e], NT, preferred_element_type=F32)
-        offset = 0 if b == 2 else 16
-        here, later = q[offset : offset + 32], q[48 + offset : 48 + offset + 32]
-        return (jnp.where(first, here, 0.0), later) if a < 2 else (here, None)
-
-    early = {}
-    for f in (1, 0):
-        terms = dict(early)
-        for a in (1,) if f else (0, 2):
-            for b in range(3):
-                for e in range(3):
-                    key = (b % 2, e)
-                    here, later = spread_og(a, b, e)
-                    if f:
-                        early[key] = early.get(key, 0.0) + here
-                        terms[key] = terms.get(key, 0.0) + later
-                    else:
-                        terms[key] = terms[key] + (here if a else here + later)
-        for b in range(2):
-            even = terms[b, 0] + move_in_16(terms[b, 2], 1)
-            odd = terms[b, 1]
-            for u in range(2):
-                hg[f, 2 * u + b, 0:16] = even[16 * u : 16 * u + 16]
-                hg[f, 2 * u + b, 16:32] = odd[16 * u : 16 * u + 16]
-        grad = (hg[f].reshape(128, 256) * zs[0, 128 * f : 128 * f + 128]).astype(BF16)
-        ge[f, 1:5] = grad.reshape(4, 32, 256)
-        for k in range(2):
-            gs[k, f] = grad[:, 128 * k : 128 * (k + 1)].reshape(4, 32, 128)
-    gather_sends(0, *g_move)
     for c in g_rows:
         c.start()
 
@@ -402,8 +404,24 @@
                 sl.at[(y + k) % ny, two], r1.at[k - 1, two],
                 rs1s.at[i, k - 1], rs1r.at[i, k - 1], at_y((y + k) % ny),
             )
-            for k in (2, 1, 3)
+            for k in (1, 3, 2)
         ]
+
+    y_far = (y + 2) % ny
+
+    def across_copy(j):
+        c = chunk_at(j)
+        k = (c - z + nz) % nz - 1
+        where = (t, c * 2 + h % 2, d)
+        return send(sl.at[y_far, j], q1.at[k], q1s.at[k], q1r.at[k], where)
+
+    across_sum = send(q2, q3, q2s.at[0], q2r.at[0], at_y(y_far))
+
+    def for_y(copies, act):
+        for copy in copies[:2]:
+            getattr(copy, act)()
+        pl.when(core == 0)(getattr(copies[2], act))
+
 
     def send_chunks(i):
         def cut(m, carry):
@@ -426,8 +444,13 @@
             return carry
 
         lax.fori_loop(0, 2 * ny, cut, 0)
-        for copy in y_copies(i):
-            copy.start()
+        for_y(y_copies(i), "start")
+
+        @pl.when(core == 1)
+        def _():
+            for j in (2 * i, 2 * i + 1):
+                if j < nz - 1:
+                    across_copy(j).start()
 
 
     for k in range(3):
@@ -468,12 +491,12 @@
         return send(s1.at[c], r2.at[k], rs2s.at[k], rs2r.at[k], where)
 
     def pass_chunks(i):
-        for copy in y_copies(i):
-            copy.wait_recv()
+        for_y(y_copies(i), "wait_recv")
         for j in (2 * i, 2 * i + 1):
             total = sl[y, j].astype(F32)
-            for n in range(ny - 1):
+            for n in (0, 2):
                 total = total + r1[n, j].astype(F32)
+            total = total + jnp.where(core == 0, r1[1, j].astype(F32), 0.0)
             s1[chunk_at(j)] = total.astype(BF16)
             if j < nz - 1:
                 z_copy(j).start()
@@ -500,6 +523,18 @@
     pass_chunks(2)
     pass_chunks(3)
 
+    @pl.when(core == 1)
+    def _():
+        total = sl[y_far, nz - 1].astype(F32)
+        for k in range(1, nz):
+            source = ((z - k + nz) % nz * 2 + h % 2, d)
+            send(
+                sl.at[y_far, 0], q1.at[k - 1], q1s.at[k - 1], q1r.at[k - 1], (t, *source)
+            ).wait_recv()
+            total = total + q1[k - 1].astype(F32)
+        q2[...] = total.astype(BF16)
+        across_sum.start()
+
     g_frames.wait_recv()
 
     @pl.when(t == nt - 1)
@@ -540,6 +575,8 @@
             s1.at[z], r2.at[k - 1], rs2s.at[k - 1], rs2r.at[k - 1], (t, *source)
         ).wait_recv()
         total = total + r2[k - 1].astype(F32)
+    pl.when(core == 1)(across_sum.wait_recv)
+    total = total + jnp.where(core == 1, q3[...].astype(F32), 0.0)
     fs[...] = total.astype(BF16)
     t_sends = []
     for k in range(1, nt):
@@ -555,10 +592,16 @@
     for c in og_halo + x_halo + [h_rows] + g_rows + [h_frames, g_frames] + t_sends:
         c.wait_send()
     for i in range(nz // 2):
-        for copy in y_copies(i):
-            copy.wait_send()
+        for_y(y_copies(i), "wait_send")
     for j in range(nz - 1):
         z_copy(j).wait_send()
+
+    @pl.when(core == 1)
+    def _():
+        for j in range(nz - 1):
+            across_copy(j).wait_send()
+        across_sum.wait_send()
+
     for move in (x_move, x_rim_move, g_move):
         gather_sent(0, *move)
     for move in (og_move, h_move):
@@ -622,11 +665,12 @@
         vm(27 * 128 + 8, 128, dtype=F32), vm(27 * 64 + 8, 256, dtype=F32),
         vm(ny, nz, slot, 128), vm(ny - 1, nz, slot, 128),
         vm(nz, slot, 128), vm(nz - 1, slot, 128),
+        vm(nz - 1, slot, 128), vm(slot, 128), vm(slot, 128),
         vm(slot, 128),
         dma((4,)), dma((8,)), dma((8,)), dma((5,)), dma((5,)),
     ]
     scratch += [dma((n,)) for _ in range(6) for n in (nt // 2, nt)]
-    scratch += [dma(n) for n in ((nz // 2, ny - 1),) * 2 + ((nz - 1,),) * 2 + ((nt - 1,),) * 2]
+    scratch += [dma(n) for n in ((nz // 2, ny - 1),) * 2 + ((nz - 1,),) * 4 + ((1,),) * 2 + ((nt - 1,),) * 2]
     vmem = pl.BlockSpec(memory_space=pltpu.VMEM)
     hbm = pl.BlockSpec(memory_space=pltpu.HBM)
     shape = jax.ShapeDtypeStruct

time: 48.4 us -> 48 us (level)
  Pallas kernels: 47.7 us -> 47.2 us
where the time goes in v4:
time: 48 us; the launch traced here: 47.9 us
  Pallas kernels  47.2 us (98%)
  between operations  0.64 us (1%)
    pallas_call x1, Pallas kernels, body(): pl.pallas_call(functools.partial(kernel, mesh_sizes), out_shape=(*feature...  46.3 us

profile of v4, /device:TPU:1, one launch (start us, length us, event | category | flops | bytes accessed | tf_op | source)
XLA Modules:
  0.0 47.9 jit_solution(5067664915798936720)
XLA Ops:
  0.6 46.3 %shard_map.75 = (bf16[32,256]{1,0:T(8,128)(2,1)S(1)}, bf16[256,256]{1,0:T(8,128)(2,1)S(1)}, bf16[8,112,128]{2,1,0:T(8,128)(2,1)S(1)}) custom-call(bf16[256,256]{1,0:T(8,128)(2,1)} %bitcast.8, bf16[27,256,256]{2,1,0:T(8,128)(2,1)} %bitcast.6, bf16[27,256,256]{2,1,0:T(8,128)(2,1)} %bitcast.7, bf16[32,256]{1,0:T(8,128)(2,1)} %bitcast.9), custom_call_target="tpu_custom_call" | custom-call | tf_op jit(solution)/shard_map/pallas_call | solution.py:678
  47.0 0.9 %shard_map.76 = (bf16[32,256]{1,0:T(8,128)(2,1)}, bf16[256,256]{1,0:T(8,128)(2,1)}, f32[216,256]{1,0:T(8,128)}, f32[216,256]{1,0:T(8,128)}) custom-call(bf16[32,256]{1,0:T(8,128)(2,1)S(1)} %get-tuple-element.11.enc_ref, bf16[256,256]{1,0:T(8,128)(2,1)S(1)} %get-tuple-element.12.clip_ref, bf16[8,112,128]{2,1,0:T(8,128)(2,1)S(1)} %get-tuple-element.13.fg), custom_call_target="tpu_custom_call" | custom-call | tf_op jit(solution)/shard_map/pallas_call | solution.py:699

commit v5 on v4

--- a/solution.py
+++ b/solution.py
@@ -171,7 +171,7 @@
     def gather_sends(role, source, target, ssem, rsem, to_h=None):
         rim = to_h is not None
         to_h = to_h if rim else h
-        for k in range(nt // 2):
+        for k in (2, 1, 3, 0):
             to_chip = (chip + k) % (nt // 2)
             to = to_chip * 2 + role
             c = send(source(to_chip), target(t), ssem.at[k], rsem.at[t], (to, to_h, d))
@@ -183,7 +183,7 @@
     def gather_sent(role, source, target, ssem, rsem, to_h=None):
         rim = to_h is not None
         to_h = to_h if rim else h
-        for k in range(nt // 2):
+        for k in (2, 1, 3, 0):
             to_chip = (chip + k) % (nt // 2)
             to = to_chip * 2 + role
             c = send(source(to_chip), target(t), ssem.at[k], rsem.at[t], (to, to_h, d))
@@ -578,16 +578,19 @@
     pl.when(core == 1)(across_sum.wait_recv)
     total = total + jnp.where(core == 1, q3[...].astype(F32), 0.0)
     fs[...] = total.astype(BF16)
-    t_sends = []
-    for k in range(1, nt):
-        where = ((t + k) % nt, h, d)
-        t_sends.append(send(fs, fg.at[t], ags.at[k - 1], agr.at[k - 1], where))
+    steps = [(k, n) for k in (2, 1, 3) for n in (0, 1)] + [(0, 1)]
+
+    def t_copy(i, sign, slot_of):
+        k, n = steps[i]
+        other = (chip + sign * k + nt // 2) % (nt // 2) * 2 + (core + n) % 2
+        return send(fs, fg.at[slot_of(other)], ags.at[i], agr.at[i], (other, h, d))
+
+    t_sends = [t_copy(i, 1, lambda other: t) for i in range(nt - 1)]
     for c in t_sends:
         c.start()
     fg[t] = fs[...]
-    for k in range(1, nt):
-        s = (t + nt - k) % nt
-        send(fs, fg.at[s], ags.at[k - 1], agr.at[k - 1], (s, h, d)).wait_recv()
+    for i in range(nt - 1):
+        t_copy(i, -1, lambda other: other).wait_recv()
 
     for c in og_halo + x_halo + [h_rows] + g_rows + [h_frames, g_frames] + t_sends:
         c.wait_send()

time: 48 us -> 47.4 us (0.987)
  Pallas kernels: 47.2 us -> 46.7 us
    pallas_call x1, Pallas kernels: 46.3 us -> 45.8 us  [body(): pl.pallas_call(functools.partial(kernel, mesh_sizes), out_shape=(*feature...]
where the time goes in v5:
time: 47.4 us; the launch traced here: 47.3 us
  Pallas kernels  46.7 us (99%)
  between operations  0.64 us (1%)
    pallas_call x1, Pallas kernels, body(): pl.pallas_call(functools.partial(kernel, mesh_sizes), out_shape=(*feature...  45.8 us

profile of v5, /device:TPU:1, one launch (start us, length us, event | category | flops | bytes accessed | tf_op | source)
XLA Modules:
  0.0 47.3 jit_solution(14436765147123530615)
XLA Ops:
  0.6 45.8 %shard_map.75 = (bf16[32,256]{1,0:T(8,128)(2,1)S(1)}, bf16[256,256]{1,0:T(8,128)(2,1)S(1)}, bf16[8,112,128]{2,1,0:T(8,128)(2,1)S(1)}) custom-call(bf16[256,256]{1,0:T(8,128)(2,1)} %bitcast.8, bf16[27,256,256]{2,1,0:T(8,128)(2,1)} %bitcast.6, bf16[27,256,256]{2,1,0:T(8,128)(2,1)} %bitcast.7, bf16[32,256]{1,0:T(8,128)(2,1)} %bitcast.9), custom_call_target="tpu_custom_call" | custom-call | tf_op jit(solution)/shard_map/pallas_call | solution.py:681
  46.4 0.9 %shard_map.76 = (bf16[32,256]{1,0:T(8,128)(2,1)}, bf16[256,256]{1,0:T(8,128)(2,1)}, f32[216,256]{1,0:T(8,128)}, f32[216,256]{1,0:T(8,128)}) custom-call(bf16[32,256]{1,0:T(8,128)(2,1)S(1)} %get-tuple-element.11.enc_ref, bf16[256,256]{1,0:T(8,128)(2,1)S(1)} %get-tuple-element.12.clip_ref, bf16[8,112,128]{2,1,0:T(8,128)(2,1)S(1)} %get-tuple-element.13.fg), custom_call_target="tpu_custom_call" | custom-call | tf_op jit(solution)/shard_map/pallas_call | solution.py:702
